TPU v7x, 32 devices: a whole 2x2x4 slice. The times are simulated.
32 devices in a mesh: dp: 8 (over z, x), ctx: 4 (over y, core).
Axes of the slice: x: 2, y: 2, z: 4, core: 2. Of those that a mesh axis runs over, the one named last changes fastest.
Arguments:
- tokens_in: bfloat16 [16, 1024, 768], P('dp', 'ctx'), may hold values from -6 to 6
- out_grad: bfloat16 [16, 1024, 768], P('dp', 'ctx'), may hold values from -6 to 6
- w_query: bfloat16 [768, 768], P(('dp', 'ctx')), may hold values from -0.3125 to 0.3125
- w_key: bfloat16 [768, 768], P(('dp', 'ctx')), may hold values from -0.21875 to 0.21875
- w_value: bfloat16 [768, 768], P(('dp', 'ctx')), may hold values from -0.21875 to 0.21875
- w_out: bfloat16 [768, 768], P(('dp', 'ctx')), may hold values from -0.875 to 0.875
- w_up: bfloat16 [768, 3072], P(('dp', 'ctx')), may hold values from -0.21875 to 0.21875
- w_down: bfloat16 [3072, 768], P(('dp', 'ctx')), may hold values from -0.109375 to 0.109375
- b_query: bfloat16 [768], P(('dp', 'ctx')), may hold values from -4 to 4
- b_value: bfloat16 [768], P(('dp', 'ctx')), may hold values from -4 to 4
- b_out: bfloat16 [768], P(('dp', 'ctx')), may hold values from -4 to 4
- b_up: bfloat16 [3072], P(('dp', 'ctx')), may hold values from -4 to 4
- b_down: bfloat16 [768], P(('dp', 'ctx')), may hold values from -4 to 4
- norm1_gain: bfloat16 [768], P(('dp', 'ctx')), may hold values from 0.25 to 1.75
- norm1_shift: bfloat16 [768], P(('dp', 'ctx')), may hold values from -4 to 4
- norm2_gain: bfloat16 [768], P(('dp', 'ctx')), may hold values from 0.25 to 1.75
- norm2_shift: bfloat16 [768], P(('dp', 'ctx')), may hold values from -4 to 4
Outputs:
- layer_out: bfloat16 [16, 1024, 768], P('dp', 'ctx')
- grad_tokens: float32 [16, 1024, 768], P('dp', 'ctx')
- grad_w_query: float32 [768, 768], P(('dp', 'ctx'))
- grad_w_key: float32 [768, 768], P(('dp', 'ctx'))
- grad_w_value: float32 [768, 768], P(('dp', 'ctx'))
- grad_w_out: float32 [768, 768], P(('dp', 'ctx'))
- grad_w_up: float32 [768, 3072], P(('dp', 'ctx'))
- grad_w_down: float32 [3072, 768], P(('dp', 'ctx'))
- grad_b_query: float32 [768], P(('dp', 'ctx'))
- grad_b_value: float32 [768], P(('dp', 'ctx'))
- grad_b_out: float32 [768], P(('dp', 'ctx'))
- grad_b_up: float32 [3072], P(('dp', 'ctx'))
- grad_b_down: float32 [768], P(('dp', 'ctx'))
- grad_norm1_gain: float32 [768], P(('dp', 'ctx'))
- grad_norm1_shift: float32 [768], P(('dp', 'ctx'))
- grad_norm2_gain: float32 [768], P(('dp', 'ctx'))
- grad_norm2_shift: float32 [768], P(('dp', 'ctx'))
All inputs are finite; a program needn't handle non-finite values.
Results may differ from a plain program's by a relative error of at most 0.017.
Values may be sent and summed in bfloat16 or wider, within the bound.
No kernel may reach another device: no remote copies, remote signals or barrier semaphores. Data moves between devices by JAX's collectives and lax.ppermute only.
A program may use at most 192 MiB of HBM per device.

v0:
```python
import jax
import jax.numpy as jnp
from jax import lax
from jax.sharding import PartitionSpec as P

HEADS = 12
DH = 64
MICRO = 2


def shifted(value, axis, by):
    peers = lax.axis_size(axis)
    return lax.ppermute(value, axis, [(i, (i + by) % peers) for i in range(peers)])


def as_sent(value):
    return jax.tree.map(lambda a: a.astype(jnp.bfloat16) if a.dtype == jnp.float32 else a, value)


def layer_norm(values, norm_gain, norm_shift):
    centre = values - jnp.mean(values, axis=-1, keepdims=True)
    spread = jnp.mean(centre * centre, axis=-1, keepdims=True)
    return centre * lax.rsqrt(spread + 1e-05) * norm_gain + norm_shift


def gelu_tanh(values):
    return (
        0.5
        * values
        * (1.0 + jnp.tanh(0.7978845608028654 * (values + 0.044715 * values * values * values)))
    )


def project(left, right):
    return jnp.einsum("scd,de->sce", left, right, preferred_element_type=jnp.float32)


def project_back(left, right):
    return jnp.einsum("sce,de->scd", left, right, preferred_element_type=jnp.float32)


def weight_grad(left, right):
    return jnp.einsum("scd,sce->de", left, right, preferred_element_type=jnp.float32)


def column_sum(values):
    return jnp.sum(values.astype(jnp.float32), axis=(0, 1))


def masked_scores(query_heads, key_full, first_pos):
    seq_count, key_len = (key_full.shape[0], key_full.shape[1])
    key_heads = key_full.reshape(seq_count, key_len, HEADS, DH)
    scores = jnp.einsum(
        "sqhd,skhd->shqk", query_heads, key_heads, preferred_element_type=jnp.float32
    )
    row_pos = first_pos + jnp.arange(query_heads.shape[1], dtype=jnp.int32)
    col_pos = jnp.arange(key_len, dtype=jnp.int32)
    allowed = row_pos[:, None] >= col_pos[None, :]
    return (jnp.where(allowed, scores, -1e30), key_heads)


def micro_step(tokens, cotangent, shards, forward_weights):
    (
        w_query,
        w_key,
        w_value,
        w_out,
        w_up,
        w_down,
        b_query,
        b_value,
        b_out,
        b_up,
        b_down,
        gain_one,
        shift_one,
        gain_two,
        shift_two,
    ) = forward_weights
    seq_count, block_rows, width = tokens.shape
    query_scale = DH ** (-0.5)
    first_pos = lax.axis_index("ctx") * block_rows
    gain_one32, shift_one32 = (gain_one.astype(jnp.float32), shift_one.astype(jnp.float32))
    gain_two32, shift_two32 = (gain_two.astype(jnp.float32), shift_two.astype(jnp.float32))
    tokens32 = tokens.astype(jnp.float32)
    normed = layer_norm(tokens32, gain_one32, shift_one32).astype(jnp.bfloat16)
    queries = ((project(normed, w_query) + b_query.astype(jnp.float32)) * query_scale).astype(
        jnp.bfloat16
    )
    keys_local = project(normed, w_key).astype(jnp.bfloat16)
    values_local = (project(normed, w_value) + b_value.astype(jnp.float32)).astype(jnp.bfloat16)
    key_full, value_full = (
        lax.all_gather(keys_local, "ctx", axis=1, tiled=True),
        lax.all_gather(values_local, "ctx", axis=1, tiled=True),
    )
    query_heads = queries.reshape(seq_count, block_rows, HEADS, DH)
    scores, key_heads = masked_scores(query_heads, key_full, first_pos)
    row_max = jnp.max(scores, axis=-1, keepdims=True)
    exp_scores = jnp.exp(scores - row_max)
    row_total = jnp.sum(exp_scores, axis=-1, keepdims=True)
    probs_low = (exp_scores / row_total).astype(jnp.bfloat16)
    value_heads = value_full.reshape(seq_count, value_full.shape[1], HEADS, DH)
    mixed_heads = jnp.einsum(
        "shqk,skhd->sqhd", probs_low, value_heads, preferred_element_type=jnp.float32
    ).reshape(seq_count, block_rows, width)
    mixed_heads = mixed_heads.astype(jnp.bfloat16)
    residual = tokens32 + project(mixed_heads, w_out) + b_out.astype(jnp.float32)
    normed_two = layer_norm(residual, gain_two32, shift_two32).astype(jnp.bfloat16)
    hidden_pre = project(normed_two, w_up) + b_up.astype(jnp.float32)
    active = gelu_tanh(hidden_pre).astype(jnp.bfloat16)
    output = (residual + project(active, w_down) + b_down.astype(jnp.float32)).astype(jnp.bfloat16)
    back_weights = (
        lax.all_gather(shards[0], ("dp", "ctx"), axis=0, tiled=True),
        lax.all_gather(shards[1], ("dp", "ctx"), axis=0, tiled=True),
        lax.all_gather(shards[2], ("dp", "ctx"), axis=0, tiled=True),
        lax.all_gather(shards[3], ("dp", "ctx"), axis=0, tiled=True),
        lax.all_gather(shards[4], ("dp", "ctx"), axis=0, tiled=True),
        lax.all_gather(shards[5], ("dp", "ctx"), axis=0, tiled=True),
        lax.all_gather(shards[6], ("dp", "ctx"), axis=0, tiled=True),
        lax.all_gather(shards[7], ("dp", "ctx"), axis=0, tiled=True),
        lax.all_gather(shards[8], ("dp", "ctx"), axis=0, tiled=True),
        lax.all_gather(shards[9], ("dp", "ctx"), axis=0, tiled=True),
        lax.all_gather(shards[10], ("dp", "ctx"), axis=0, tiled=True),
        lax.all_gather(shards[11], ("dp", "ctx"), axis=0, tiled=True),
        lax.all_gather(shards[12], ("dp", "ctx"), axis=0, tiled=True),
        lax.all_gather(shards[13], ("dp", "ctx"), axis=0, tiled=True),
        lax.all_gather(shards[14], ("dp", "ctx"), axis=0, tiled=True),
    )
    w_query, w_key, w_value, w_out, w_up, w_down = back_weights[:6]
    grad_active = project_back(cotangent, w_down)
    _, gelu_pull = jax.vjp(gelu_tanh, hidden_pre)
    grad_pre = gelu_pull(grad_active)[0].astype(jnp.bfloat16)
    grad_normed_two = project_back(grad_pre, w_up)
    _, norm_pull_two = jax.vjp(layer_norm, residual, gain_two32, shift_two32)
    grad_res_part, grad_gain_two, grad_shift_two = norm_pull_two(grad_normed_two)
    grad_residual = cotangent.astype(jnp.float32) + grad_res_part
    grad_branch = grad_residual.astype(jnp.bfloat16)
    grad_mixed = project_back(grad_branch, w_out).astype(jnp.bfloat16)
    key_full, value_full = (
        lax.all_gather(keys_local, "ctx", axis=1, tiled=True),
        lax.all_gather(values_local, "ctx", axis=1, tiled=True),
    )
    value_heads = value_full.reshape(seq_count, value_full.shape[1], HEADS, DH)
    scores, key_heads = masked_scores(query_heads, key_full, first_pos)
    probs = jnp.exp(scores - row_max) / row_total
    probs_low = probs.astype(jnp.bfloat16)
    grad_heads = grad_mixed.reshape(seq_count, block_rows, HEADS, DH)
    grad_probs = jnp.einsum(
        "sqhd,skhd->shqk", grad_heads, value_heads, preferred_element_type=jnp.float32
    )
    inner_rows = jnp.sum(probs * grad_probs, axis=-1, keepdims=True)
    grad_scores = (probs * (grad_probs - inner_rows)).astype(jnp.bfloat16)
    grad_queries = jnp.einsum(
        "shqk,skhd->sqhd", grad_scores, key_heads, preferred_element_type=jnp.float32
    )
    grad_queries = grad_queries.reshape(seq_count, block_rows, width).astype(jnp.bfloat16)
    query_grad = grad_queries * query_scale

    def key_terms(first_row, row_count):
        score_part = lax.dynamic_slice_in_dim(grad_scores, first_row, row_count, 3)
        prob_part = lax.dynamic_slice_in_dim(probs_low, first_row, row_count, 3)
        key_part = jnp.einsum(
            "shqk,sqhd->kshd", score_part, query_heads, preferred_element_type=jnp.float32
        )
        value_part = jnp.einsum(
            "shqk,sqhd->kshd", prob_part, grad_heads, preferred_element_type=jnp.float32
        )
        return jnp.concatenate(
            (
                key_part.reshape(row_count, seq_count, width),
                value_part.reshape(row_count, seq_count, width),
            ),
            axis=2,
        )

    cycle_size = lax.axis_size("ctx")
    own_index = lax.axis_index("ctx")

    def carry_step(step, carried):
        holder = (own_index - step) % cycle_size
        carried = carried + key_terms(holder * block_rows, block_rows)
        return shifted(carried.astype(jnp.bfloat16), "ctx", 1).astype(carried.dtype)

    start_sums = jnp.zeros((block_rows, seq_count, 2 * width), jnp.float32)
    key_sums = lax.fori_loop(0, cycle_size, carry_step, start_sums)
    key_sums = jnp.transpose(key_sums, (1, 0, 2))
    grad_keys = key_sums[:, :, :width].astype(jnp.bfloat16)
    grad_values = key_sums[:, :, width:].astype(jnp.bfloat16)
    grad_normed = (
        project_back(query_grad, w_query)
        + project_back(grad_keys, w_key)
        + project_back(grad_values, w_value)
    )
    _, norm_pull_one = jax.vjp(layer_norm, tokens32, gain_one32, shift_one32)
    grad_tok_part, grad_gain_one, grad_shift_one = norm_pull_one(grad_normed)
    grad_tokens = grad_residual + grad_tok_part
    small_grads = (grad_gain_one, grad_shift_one, grad_gain_two, grad_shift_two)
    operands = (
        normed,
        query_grad,
        grad_keys,
        grad_values,
        mixed_heads,
        grad_branch,
        normed_two,
        grad_pre,
        active,
        cotangent,
    )
    return (output, grad_tokens, small_grads, operands)


def owner_sum(grads):
    dp_count = lax.axis_size("dp")
    ctx_count = lax.axis_size("ctx")
    blocks = tuple((grad_part.reshape(dp_count, ctx_count, -1) for grad_part in grads))
    first_section = jax.tree.map(
        lambda part, own: part.astype(own.dtype),
        lax.all_to_all(as_sent(blocks), "ctx", split_axis=1, concat_axis=1, tiled=True),
        blocks,
    )
    partial_sums = tuple((jnp.sum(piece, axis=1, keepdims=True) for piece in first_section))
    second_section = jax.tree.map(
        lambda part, own: part.astype(own.dtype),
        lax.all_to_all(as_sent(partial_sums), "dp", split_axis=0, concat_axis=0, tiled=True),
        partial_sums,
    )
    owned = []
    for grad_part, piece in zip(grads, second_section):
        summed = jnp.sum(piece, axis=(0, 1))
        row_count = grad_part.shape[0] // (dp_count * ctx_count)
        owned.append(summed.reshape((row_count,) + grad_part.shape[1:]))
    return owned


def on_device(
    tokens_in,
    out_grad,
    w_query,
    w_key,
    w_value,
    w_out,
    w_up,
    w_down,
    b_query,
    b_value,
    b_out,
    b_up,
    b_down,
    norm1_gain,
    norm1_shift,
    norm2_gain,
    norm2_shift,
):
    shards = (
        w_query,
        w_key,
        w_value,
        w_out,
        w_up,
        w_down,
        b_query,
        b_value,
        b_out,
        b_up,
        b_down,
        norm1_gain,
        norm1_shift,
        norm2_gain,
        norm2_shift,
    )
    per_micro = tokens_in.shape[0] // MICRO
    outputs = []
    grads_in = []
    operand_lists = []
    small_total = None
    for micro_index in range(MICRO):
        lower = micro_index * per_micro
        tokens = tokens_in[lower : lower + per_micro]
        cotangent = out_grad[lower : lower + per_micro]
        forward_weights = (
            lax.all_gather(shards[0], ("dp", "ctx"), axis=0, tiled=True),
            lax.all_gather(shards[1], ("dp", "ctx"), axis=0, tiled=True),
            lax.all_gather(shards[2], ("dp", "ctx"), axis=0, tiled=True),
            lax.all_gather(shards[3], ("dp", "ctx"), axis=0, tiled=True),
            lax.all_gather(shards[4], ("dp", "ctx"), axis=0, tiled=True),
            lax.all_gather(shards[5], ("dp", "ctx"), axis=0, tiled=True),
            lax.all_gather(shards[6], ("dp", "ctx"), axis=0, tiled=True),
            lax.all_gather(shards[7], ("dp", "ctx"), axis=0, tiled=True),
            lax.all_gather(shards[8], ("dp", "ctx"), axis=0, tiled=True),
            lax.all_gather(shards[9], ("dp", "ctx"), axis=0, tiled=True),
            lax.all_gather(shards[10], ("dp", "ctx"), axis=0, tiled=True),
            lax.all_gather(shards[11], ("dp", "ctx"), axis=0, tiled=True),
            lax.all_gather(shards[12], ("dp", "ctx"), axis=0, tiled=True),
            lax.all_gather(shards[13], ("dp", "ctx"), axis=0, tiled=True),
            lax.all_gather(shards[14], ("dp", "ctx"), axis=0, tiled=True),
        )
        output, grad_tokens, small_grads, operands = micro_step(
            tokens, cotangent, shards, forward_weights
        )
        outputs.append(output)
        grads_in.append(grad_tokens)
        operand_lists.append(operands)
        if small_total is None:
            small_total = small_grads
        else:
            small_total = tuple(
                (total_grad + update for total_grad, update in zip(small_total, small_grads))
            )
    joined = tuple(
        (jnp.concatenate([entry[index] for entry in operand_lists], axis=0) for index in range(10))
    )
    (
        normed,
        query_grad,
        grad_keys,
        grad_values,
        mixed_heads,
        grad_branch,
        normed_two,
        grad_pre,
        active,
        cotangent,
    ) = joined
    grads = (
        weight_grad(normed, query_grad),
        weight_grad(normed, grad_keys),
        weight_grad(normed, grad_values),
        weight_grad(mixed_heads, grad_branch),
        weight_grad(normed_two, grad_pre),
        weight_grad(active, cotangent),
        column_sum(query_grad),
        column_sum(grad_values),
        column_sum(grad_branch),
        column_sum(grad_pre),
        column_sum(cotangent),
        small_total[0],
        small_total[1],
        small_total[2],
        small_total[3],
    )
    owned = owner_sum(grads)
    layer_out = jnp.concatenate(outputs, axis=0)
    grad_tokens_all = jnp.concatenate(grads_in, axis=0)
    return (
        layer_out,
        grad_tokens_all,
        owned[0],
        owned[1],
        owned[2],
        owned[3],
        owned[4],
        owned[5],
        owned[6],
        owned[7],
        owned[8],
        owned[9],
        owned[10],
        owned[11],
        owned[12],
        owned[13],
        owned[14],
    )


def solution(mesh):
    placed = (
        P("dp", "ctx", None),
        P("dp", "ctx", None),
        P(("dp", "ctx"), None),
        P(("dp", "ctx"), None),
        P(("dp", "ctx"), None),
        P(("dp", "ctx"), None),
        P(("dp", "ctx"), None),
        P(("dp", "ctx"), None),
        P(("dp", "ctx")),
        P(("dp", "ctx")),
        P(("dp", "ctx")),
        P(("dp", "ctx")),
        P(("dp", "ctx")),
        P(("dp", "ctx")),
        P(("dp", "ctx")),
        P(("dp", "ctx")),
        P(("dp", "ctx")),
    )
    return jax.shard_map(
        on_device,
        mesh=mesh,
        in_specs=placed,
        out_specs=(
            P("dp", "ctx", None),
            P("dp", "ctx", None),
            P(("dp", "ctx"), None),
            P(("dp", "ctx"), None),
            P(("dp", "ctx"), None),
            P(("dp", "ctx"), None),
            P(("dp", "ctx"), None),
            P(("dp", "ctx"), None),
            P(("dp", "ctx")),
            P(("dp", "ctx")),
            P(("dp", "ctx")),
            P(("dp", "ctx")),
            P(("dp", "ctx")),
            P(("dp", "ctx")),
            P(("dp", "ctx")),
            P(("dp", "ctx")),
            P(("dp", "ctx")),
        ),
        check_vma=False,
    )
```

profile of v0, /device:TPU:0, one launch (start us, length us, event | category | flops | bytes accessed | tf_op | source)
XLA Modules:
  0.0 1150.0 jit_solution(7695446279525502493)
XLA Ops:
  17.0 42.7 %all-reduce.9 = (bf16[768]{0:T(1024)(128)(2,1)S(1)}, bf16[768]{0:T(1024)(128)(2,1)S(1)}, bf16[768]{0:T(1024)(128)(2,1)S(1)}, bf16[768]{0:T(1024)(128)(2,1)}, bf1...) all-reduce(bf16[768]{0:T(1024)(128)(2,1)S(1)} %dynamic-update-slice, ...), channel_id=1, replica_groups=mesh['dp'=8,'ctx'=4] {'dp','ctx'}, use_global_device_ids=true, to_apply=%add.1 | all-reduce | flops 9216 | bytes 36864
  70.7 53.2 %all-gather.15.cloned.1.call-done = bf16[768,768]{1,0:T(8,128)(2,1)} async-done(((bf16[24,768]{1,0:T(8,128)(2,1)}), bf16[768,768]{1,0:T(8,128)(2,1)}) %all-gather.15.cloned.1.call-update) | async-done | bytes 1179664 | tf_op jit(solution)/shard_map/all_gather | solution.py:284
  143.9 4.4 all-to-all-start.21
  148.3 31.6 %all-gather.17.cloned.1.call-done = bf16[768,768]{1,0:T(8,128)(2,1)} async-done(((bf16[24,768]{1,0:T(8,128)(2,1)}), bf16[768,768]{1,0:T(8,128)(2,1)}) %all-gather.17.cloned.1.call-update) | async-done | bytes 1179664 | tf_op jit(solution)/shard_map/all_gather | solution.py:282
  188.1 11.8 %all-gather.29.cloned.1.call-done = bf16[1024,768]{1,0:T(8,128)(2,1)} async-done(((bf16[256,768]{1,0:T(8,128)(2,1)}), bf16[1024,768]{1,0:T(8,128)(2,1)}) %all-gather.29.cloned.1.call-update) | async-done | bytes 1572880 | tf_op jit(solution)/shard_map/all_gather | solution.py:93
  202.5 18.5 %all-gather.27.cloned.1.call-done = bf16[1024,768]{1,0:T(8,128)(2,1)} async-done(((bf16[256,768]{1,0:T(8,128)(2,1)}), bf16[1024,768]{1,0:T(8,128)(2,1)}) %all-gather.27.cloned.1.call-update) | async-done | bytes 1572880 | tf_op jit(solution)/shard_map/all_gather | solution.py:94
  223.6 19.1 %all-gather.31.cloned.1.call-done = bf16[1024,768]{1,0:T(8,128)(2,1)} async-done(((bf16[256,768]{1,0:T(8,128)(2,1)}), bf16[1024,768]{1,0:T(8,128)(2,1)}) %all-gather.31.cloned.1.call-update) | async-done | bytes 1572880 | tf_op jit(solution)/shard_map/all_gather | solution.py:94
  245.3 18.7 %all-gather.33.cloned.1.call-done = bf16[1024,768]{1,0:T(8,128)(2,1)} async-done(((bf16[256,768]{1,0:T(8,128)(2,1)}), bf16[1024,768]{1,0:T(8,128)(2,1)}) %all-gather.33.cloned.1.call-update) | async-done | bytes 1572880 | tf_op jit(solution)/shard_map/all_gather | solution.py:93
  266.8 10.0 fusion.180
  276.8 8.0 fusion.73
  284.8 36.3 %all-gather.21.cloned.1.call-done = bf16[768,768]{1,0:T(8,128)(2,1)} async-done(((bf16[24,768]{1,0:T(8,128)(2,1)}), bf16[768,768]{1,0:T(8,128)(2,1)}) %all-gather.21.cloned.1.call-update) | async-done | bytes 1179664 | tf_op jit(solution)/shard_map/all_gather | solution.py:285
  324.3 10.2 fusion.181
  334.4 7.7 fusion.70
  345.9 40.7 %all-gather.23.cloned.1.call-done = bf16[768,3072]{1,0:T(8,128)(2,1)} async-done(((bf16[24,3072]{1,0:T(8,128)(2,1)}), bf16[768,3072]{1,0:T(8,128)(2,1)}) %all-gather.23.cloned.1.call-update) | async-done | bytes 4718608 | tf_op jit(solution)/shard_map/all_gather | solution.py:286
  386.5 5.6 convolution_add_fusion.1
  395.2 56.5 %all-gather.25.cloned.1.call-done = bf16[3072,768]{1,0:T(8,128)(2,1)} async-done(((bf16[96,768]{1,0:T(8,128)(2,1)}), bf16[3072,768]{1,0:T(8,128)(2,1)}) %all-gather.25.cloned.1.call-update) | async-done | bytes 4718608 | tf_op jit(solution)/shard_map/all_gather | solution.py:287
  451.7 7.6 fusion.184
  459.3 4.5 fusion.185
  480.3 8.7 convert_bitcast_fusion
  489.0 6.0 multiply_convert_fusion
  498.4 72.5 %while.33 = (s32[]{:T(128)}, f32[256,1,1536]{0,2,1:T(8,128)S(1)}, s32[]{:T(128)}, bf16[1,12,256,1024]{3,2,1,0:T(8,128)(2,1)}, bf16[1,256,12,64]{1,3,2,0:T(8,128)...) while((s32[]{:T(128)}, f32[256,1,1536]{0,2,1:T(8,128)S(1)}, ...), condition=%wide.region_23.24_spmd.clone, body=%wide.region_22.23_spmd.clone.sunk | while | flops 203292688 | bytes 14942558 | solution.py:185
  503.7 11.5 collective-permute-done.1
  521.5 11.7 %collective-permute-done.1 = bf16[256,1,1536]{0,2,1:T(8,128)(2,1)} collective-permute-done((bf16[256,1,1536]{0,2,1:T(8,128)(2,1)}, bf16[256,1,1536]{0,2,1:T(8,128)(2,1)}, u32[]{:S(2)}, u32[]{:S(2)}) %collective-permute-start.1) | collective-permute-done | bytes 786464 | tf_op jit(solution)/shard_map/while/body/eval_jaxpr/ppermute | solution.py:13
  539.6 11.7 %collective-permute-done.1 = bf16[256,1,1536]{0,2,1:T(8,128)(2,1)} collective-permute-done((bf16[256,1,1536]{0,2,1:T(8,128)(2,1)}, bf16[256,1,1536]{0,2,1:T(8,128)(2,1)}, u32[]{:S(2)}, u32[]{:S(2)}) %collective-permute-start.1) | collective-permute-done | bytes 786464 | tf_op jit(solution)/shard_map/while/body/eval_jaxpr/ppermute | solution.py:13
  557.7 11.7 %collective-permute-done.1 = bf16[256,1,1536]{0,2,1:T(8,128)(2,1)} collective-permute-done((bf16[256,1,1536]{0,2,1:T(8,128)(2,1)}, bf16[256,1,1536]{0,2,1:T(8,128)(2,1)}, u32[]{:S(2)}, u32[]{:S(2)}) %collective-permute-start.1) | collective-permute-done | bytes 786464 | tf_op jit(solution)/shard_map/while/body/eval_jaxpr/ppermute | solution.py:13
  575.3 8.7 convert_bitcast_fusion.1
  584.0 6.0 multiply_convert_fusion.1
  593.4 62.8 %while.32 = (s32[]{:T(128)}, f32[256,1,1536]{0,2,1:T(8,128)S(1)}, s32[]{:T(128)}, bf16[1,12,256,1024]{3,2,1,0:T(8,128)(2,1)}, bf16[1,256,12,64]{1,3,2,0:T(8,128)...) while((s32[]{:T(128)}, f32[256,1,1536]{0,2,1:T(8,128)S(1)}, ...), condition=%wide.region_16.17_spmd.clone, body=%wide.region_15.16_spmd.clone.sunk | while | flops 203292688 | bytes 14942558 | solution.py:185
  597.5 11.4 collective-permute-done
  613.2 11.4 collective-permute-done
  629.0 11.4 collective-permute-done
  644.7 11.4 collective-permute-done
  716.7 4.3 all-to-all-start.27
  722.3 5.1 all-to-all-done.27
  731.3 5.7 all-to-all-done.29
  741.0 5.7 all-to-all-done.17
  750.6 5.7 all-to-all-done.25
  760.7 5.3 all-to-all-done.15
  770.1 5.6 all-to-all-done.13
  786.6 5.7 all-to-all-done.23
  835.4 7.0 all-to-all-done
  855.5 7.0 all-to-all-done.4
  862.5 4.3 all-to-all-start.2
  871.0 11.7 %all-to-all-done.2 = bf16[8,4,18432]{2,0,1:T(8,128)(2,1)} async-done(((bf16[8,4,18432]{2,0,1:T(8,128)(2,1)}), bf16[8,4,18432]{2,0,1:T(8,128)(2,1)}, u32[]{:S(2)}, u32[]{:S(2)}) %all-to-all-start.2) | async-done | bytes 1179680 | tf_op jit(solution)/shard_map/all_to_all | solution.py:219
  882.8 5.9 all-to-all-start.7
  892.0 6.1 all-to-all-done.7
  905.0 5.8 all-to-all-done.1
  932.1 4.3 bitcast_convert_fusion
  936.4 8.3 convert_element_type.701
  944.7 7.1 copy.138
  952.5 5.2 all-to-all-start.10
  957.6 7.0 bitcast_convert_fusion.1
  964.7 8.3 convert_element_type.695
  972.9 7.2 copy.135
  980.1 31.4 %all-to-all-done.10 = bf16[8,4,73728]{2,0,1:T(8,128)(2,1)} async-done(((bf16[8,4,73728]{2,0,1:T(8,128)(2,1)}), bf16[8,4,73728]{2,0,1:T(8,128)(2,1)}, u32[]{:S(2)}, u32[]{:S(2)}) %all-to-all-start.10) | async-done | bytes 4718624 | tf_op jit(solution)/shard_map/all_to_all | solution.py:219
  1011.5 5.0 all-to-all-start.8
  1017.7 4.4 reduce_sum.786
  1028.9 41.4 %all-to-all-done.8 = bf16[8,4,73728]{2,0,1:T(8,128)(2,1)} async-done(((bf16[8,4,73728]{2,0,1:T(8,128)(2,1)}), bf16[8,4,73728]{2,0,1:T(8,128)(2,1)}, u32[]{:S(2)}, u32[]{:S(2)}) %all-to-all-start.8) | async-done | bytes 4718624 | tf_op jit(solution)/shard_map/all_to_all | solution.py:219
  1070.3 6.3 all-to-all-start.11
  1080.3 5.2 fusion.77
  1085.5 5.1 fusion.76
  1098.1 6.9 all-to-all-done.11
  1122.3 4.4 reshape.1107
  1132.2 5.4 all-to-all-done.9
  (541 shorter events, 370.7 us)
Async XLA Ops:
  7.2 60.9 %all-gather.19.cloned.1.call-start = ((), (), s32[]{:S(2)}) async-start(), calls=%async_computation.32 | async-start | bytes 1216512 | tf_op jit(solution)/shard_map/all_gather | solution.py:283
  7.9 116.0 %all-gather.15.cloned.1.call-start = ((), (), s32[]{:S(2)}) async-start(), calls=%async_computation.30 | async-start | bytes 1216512 | tf_op jit(solution)/shard_map/all_gather | solution.py:284
  8.7 171.2 %all-gather.17.cloned.1.call-start = ((), (), s32[]{:S(2)}) async-start(), calls=%async_computation.31 | async-start | bytes 1216512 | tf_op jit(solution)/shard_map/all_gather | solution.py:282
  9.4 190.5 %all-gather.29.cloned.1.call-start = ((), (), s32[]{:S(2)}) async-start(), calls=%async_computation.37 | async-start | bytes 1966080 | tf_op jit(solution)/shard_map/all_gather | solution.py:93
  59.7 66.7 %copy-start.49 = (f32[768]{0:T(1024)}, f32[768]{0:T(1024)S(1)}, u32[]{:S(2)}) copy-start(f32[768]{0:T(1024)S(1)} %convert_element_type.620) | copy-start | bytes 9220
  61.0 65.4 %copy-start.55 = (f32[256]{0:T(256)}, f32[256]{0:T(256)S(1)}, u32[]{:S(2)}) copy-start(f32[256]{0:T(256)S(1)} %broadcast_multiply_fusion.3) | copy-start | bytes 3076
  61.0 65.4 %copy-start.57 = (f32[256]{0:T(256)}, f32[256]{0:T(256)S(1)}, u32[]{:S(2)}) copy-start(f32[256]{0:T(256)S(1)} %broadcast_multiply_fusion.1) | copy-start | bytes 3076
  63.0 63.4 %copy-start.61 = (f32[256]{0:T(256)}, f32[256]{0:T(256)S(1)}, u32[]{:S(2)}) copy-start(f32[256]{0:T(256)S(1)} %fusion.154) | copy-start | bytes 3076
  63.1 63.4 %copy-start.63 = (f32[256]{0:T(256)}, f32[256]{0:T(256)S(1)}, u32[]{:S(2)}) copy-start(f32[256]{0:T(256)S(1)} %fusion.156) | copy-start | bytes 3076
  64.6 64.6 %copy-start.33 = (bf16[1,256,768]{2,1,0:T(8,128)(2,1)}, bf16[1,256,768]{2,1,0:T(8,128)(2,1)S(1)}, u32[]{:S(2)}) copy-start(bf16[1,256,768]{2,1,0:T(8,128)(2,1)S(1)} %get-tuple-element.503) | copy-start | bytes 1179652
  64.6 115.3 %copy-start.32 = (bf16[1,256,768]{2,1,0:T(8,128)(2,1)}, bf16[1,256,768]{2,1,0:T(8,128)(2,1)S(1)}, u32[]{:S(2)}) copy-start(bf16[1,256,768]{2,1,0:T(8,128)(2,1)S(1)} %get-tuple-element.502) | copy-start | bytes 1179652
  70.6 58.6 %copy-start.4 = (bf16[768,768]{1,0:T(8,128)(2,1)S(1)}, bf16[768,768]{1,0:T(8,128)(2,1)}, u32[]{:S(2)}) copy-start(bf16[768,768]{1,0:T(8,128)(2,1)} %all-gather.19.cloned.1.call-done) | copy-start | bytes 3538948
  70.6 150.4 %all-gather.27.cloned.1.call-start = ((), (), s32[]{:S(2)}) async-start(), calls=%async_computation.36 | async-start | bytes 1966080 | tf_op jit(solution)/shard_map/all_gather | solution.py:94
  126.5 116.2 %all-gather.31.cloned.1.call-start = ((), (), s32[]{:S(2)}) async-start(), calls=%async_computation.38 | async-start | bytes 1966080 | tf_op jit(solution)/shard_map/all_gather | solution.py:94
  129.1 134.9 %all-gather.33.cloned.1.call-start = ((), (), s32[]{:S(2)}) async-start(), calls=%async_computation.39 | async-start | bytes 1966080 | tf_op jit(solution)/shard_map/all_gather | solution.py:93
  130.4 190.6 %all-gather.21.cloned.1.call-start = ((), (), s32[]{:S(2)}) async-start(), calls=%async_computation.33 | async-start | bytes 1216512 | tf_op jit(solution)/shard_map/all_gather | solution.py:285
  131.2 255.3 %all-gather.23.cloned.1.call-start = ((), (), s32[]{:S(2)}) async-start(), calls=%async_computation.34 | async-start | bytes 4866048 | tf_op jit(solution)/shard_map/all_gather | solution.py:286
  131.9 319.8 %all-gather.25.cloned.1.call-start = ((), (), s32[]{:S(2)}) async-start(), calls=%async_computation.35 | async-start | bytes 4866048 | tf_op jit(solution)/shard_map/all_gather | solution.py:287
  133.4 9.9 all-to-all-start.20
  143.9 521.6 %all-to-all-start.21 = ((bf16[8,1,24]{2,1,0:T(2,128)(2,1)}), bf16[8,1,24]{2,1,0:T(2,128)(2,1)}, u32[]{:S(2)}, u32[]{:S(2)}) async-start(bf16[8,1,24]{2,1,0:T(2,128)(2,1)} %copy.149), calls=%async_computation.21 | async-start | bytes 8192 | tf_op jit(solution)/shard_map/all_to_all | solution.py:225
  188.1 78.7 %copy-start.6 = (bf16[256,768]{0,1:T(8,128)(2,1)}, bf16[256,768]{0,1:T(8,128)(2,1)S(1)}, u32[]{:S(2)}) copy-start(bf16[256,768]{0,1:T(8,128)(2,1)S(1)} %copy.111) | copy-start | bytes 1179652
  503.4 11.7 %collective-permute-start.1 = (bf16[256,1,1536]{0,2,1:T(8,128)(2,1)}, bf16[256,1,1536]{0,2,1:T(8,128)(2,1)}, u32[]{:S(2)}, u32[]{:S(2)}) collective-permute-start(bf16[256,1,1536]{0,2,1:T(8,128)(2,1)} %fusion.268), channel_id=1, source_target_pairs={{0,1},{1,2},{2,3},{3,0},{4,5},{5,6},{6,7},{7,4},{8,9},{9,10},{10,1... | collective-permute-start | bytes 2359304 | tf_op jit(solution)/shard_map/while/body/eval_jaxpr/ppermute | solution.py:13
  521.5 11.7 %collective-permute-start.1 = (bf16[256,1,1536]{0,2,1:T(8,128)(2,1)}, bf16[256,1,1536]{0,2,1:T(8,128)(2,1)}, u32[]{:S(2)}, u32[]{:S(2)}) collective-permute-start(bf16[256,1,1536]{0,2,1:T(8,128)(2,1)} %fusion.268), channel_id=1, source_target_pairs={{0,1},{1,2},{2,3},{3,0},{4,5},{5,6},{6,7},{7,4},{8,9},{9,10},{10,1... | collective-permute-start | bytes 2359304 | tf_op jit(solution)/shard_map/while/body/eval_jaxpr/ppermute | solution.py:13
  539.6 11.7 %collective-permute-start.1 = (bf16[256,1,1536]{0,2,1:T(8,128)(2,1)}, bf16[256,1,1536]{0,2,1:T(8,128)(2,1)}, u32[]{:S(2)}, u32[]{:S(2)}) collective-permute-start(bf16[256,1,1536]{0,2,1:T(8,128)(2,1)} %fusion.268), channel_id=1, source_target_pairs={{0,1},{1,2},{2,3},{3,0},{4,5},{5,6},{6,7},{7,4},{8,9},{9,10},{10,1... | collective-permute-start | bytes 2359304 | tf_op jit(solution)/shard_map/while/body/eval_jaxpr/ppermute | solution.py:13
  557.7 11.7 %collective-permute-start.1 = (bf16[256,1,1536]{0,2,1:T(8,128)(2,1)}, bf16[256,1,1536]{0,2,1:T(8,128)(2,1)}, u32[]{:S(2)}, u32[]{:S(2)}) collective-permute-start(bf16[256,1,1536]{0,2,1:T(8,128)(2,1)} %fusion.268), channel_id=1, source_target_pairs={{0,1},{1,2},{2,3},{3,0},{4,5},{5,6},{6,7},{7,4},{8,9},{9,10},{10,1... | collective-permute-start | bytes 2359304 | tf_op jit(solution)/shard_map/while/body/eval_jaxpr/ppermute | solution.py:13
  597.5 11.5 collective-permute-start
  613.2 11.5 collective-permute-start
  628.9 11.5 collective-permute-start
  644.6 11.5 collective-permute-start
  665.5 7.0 all-to-all-start.26
  673.1 8.3 all-to-all-start.28
  677.0 119.2 %copy-start.35 = (bf16[1,256,768]{2,1,0:T(8,128)(2,1)S(1)}, bf16[1,256,768]{2,1,0:T(8,128)(2,1)}, u32[]{:S(2)}) copy-start(bf16[1,256,768]{2,1,0:T(8,128)(2,1)} %copy-done.34) | copy-start | bytes 1179652
  679.9 89.4 %copy-start.106 = (bf16[3072]{0:T(1024)(128)(2,1)S(1)}, bf16[3072]{0:T(1024)(128)(2,1)}, u32[]{:S(2)}) copy-start(bf16[3072]{0:T(1024)(128)(2,1)} %get-tuple-element.532) | copy-start | bytes 18436
  680.0 89.4 %copy-start.107 = (bf16[3072]{0:T(1024)(128)(2,1)S(1)}, bf16[3072]{0:T(1024)(128)(2,1)}, u32[]{:S(2)}) copy-start(bf16[3072]{0:T(1024)(128)(2,1)} %get-tuple-element.534) | copy-start | bytes 18436
  680.0 116.2 %copy-start.36 = (bf16[1,256,768]{2,1,0:T(8,128)(2,1)S(1)}, bf16[1,256,768]{2,1,0:T(8,128)(2,1)}, u32[]{:S(2)}) copy-start(bf16[1,256,768]{2,1,0:T(8,128)(2,1)} %get-tuple-element.511) | copy-start | bytes 1179652
  681.5 7.1 all-to-all-start.16
  688.6 7.0 all-to-all-start.24
  695.6 7.0 all-to-all-start.14
  702.6 7.0 all-to-all-start.12
  709.7 7.0 all-to-all-start.22
  716.7 10.7 all-to-all-start.27
  727.4 9.6 all-to-all-start.29
  737.0 9.6 all-to-all-start.17
  746.7 9.6 all-to-all-start.25
  756.3 9.6 all-to-all-start.15
  766.0 9.6 all-to-all-start.13
  775.6 7.0 all-to-all-start.18
  782.7 9.6 all-to-all-start.23
  792.3 10.5 all-to-all-start.19
  802.8 19.4 %all-to-all-start.6 = ((bf16[8,4,18432]{2,0,1:T(8,128)(2,1)}), bf16[8,4,18432]{2,0,1:T(8,128)(2,1)S(1)}, u32[]{:S(2)}, u32[]{:S(2)}) async-start(bf16[8,4,18432]{2,0,1:T(8,128)(2,1)} %copy.132), calls=%async_computation.6 | async-start | bytes 2359296 | tf_op jit(solution)/shard_map/all_to_all | solution.py:219
  822.1 20.2 %all-to-all-start = ((bf16[8,4,18432]{2,0,1:T(8,128)(2,1)}), bf16[8,4,18432]{2,0,1:T(8,128)(2,1)}, u32[]{:S(2)}, u32[]{:S(2)}) async-start(bf16[8,4,18432]{2,0,1:T(8,128)(2,1)} %copy.124), calls=%async_computation | async-start | bytes 2359296 | tf_op jit(solution)/shard_map/all_to_all | solution.py:219
  842.3 20.2 %all-to-all-start.4 = ((bf16[8,4,18432]{2,0,1:T(8,128)(2,1)}), bf16[8,4,18432]{2,0,1:T(8,128)(2,1)}, u32[]{:S(2)}, u32[]{:S(2)}) async-start(bf16[8,4,18432]{2,0,1:T(8,128)(2,1)} %copy.130), calls=%async_computation.4 | async-start | bytes 2359296 | tf_op jit(solution)/shard_map/all_to_all | solution.py:219
  862.5 20.2 %all-to-all-start.2 = ((bf16[8,4,18432]{2,0,1:T(8,128)(2,1)}), bf16[8,4,18432]{2,0,1:T(8,128)(2,1)}, u32[]{:S(2)}, u32[]{:S(2)}) async-start(bf16[8,4,18432]{2,0,1:T(8,128)(2,1)} %copy.127), calls=%async_computation.2 | async-start | bytes 2359296 | tf_op jit(solution)/shard_map/all_to_all | solution.py:219
  882.8 15.3 %all-to-all-start.7 = ((bf16[8,2,9216]{2,1,0:T(2,128)(2,1)}), bf16[8,2,9216]{2,1,0:T(2,128)(2,1)S(1)}, u32[]{:S(2)}, u32[]{:S(2)}) async-start(bf16[8,2,9216]{2,1,0:T(2,128)(2,1)} %reshape.1102), calls=%async_computation.7 | async-start | bytes 589824 | tf_op jit(solution)/shard_map/all_to_all | solution.py:225
  898.1 12.8 %all-to-all-start.1 = ((bf16[8,2,9216]{2,1,0:T(2,128)(2,1)}), bf16[8,2,9216]{2,1,0:T(2,128)(2,1)S(1)}, u32[]{:S(2)}, u32[]{:S(2)}) async-start(bf16[8,2,9216]{2,1,0:T(2,128)(2,1)} %reshape.1096), calls=%async_computation.1 | async-start | bytes 589824 | tf_op jit(solution)/shard_map/all_to_all | solution.py:225
  910.8 13.0 %all-to-all-start.5 = ((bf16[8,2,9216]{2,1,0:T(2,128)(2,1)}), bf16[8,2,9216]{2,1,0:T(2,128)(2,1)S(1)}, u32[]{:S(2)}, u32[]{:S(2)}) async-start(bf16[8,2,9216]{2,1,0:T(2,128)(2,1)} %reshape.1100), calls=%async_computation.5 | async-start | bytes 589824 | tf_op jit(solution)/shard_map/all_to_all | solution.py:225
  924.5 27.2 %all-to-all-start.3 = ((bf16[8,2,9216]{2,1,0:T(2,128)(2,1)}), bf16[8,2,9216]{2,1,0:T(2,128)(2,1)S(1)}, u32[]{:S(2)}, u32[]{:S(2)}) async-start(bf16[8,2,9216]{2,1,0:T(2,128)(2,1)} %reshape.1098), calls=%async_computation.3 | async-start | bytes 589824 | tf_op jit(solution)/shard_map/all_to_all | solution.py:225
  952.5 59.0 %all-to-all-start.10 = ((bf16[8,4,73728]{2,0,1:T(8,128)(2,1)}), bf16[8,4,73728]{2,0,1:T(8,128)(2,1)}, u32[]{:S(2)}, u32[]{:S(2)}) async-start(bf16[8,4,73728]{2,0,1:T(8,128)(2,1)} %copy.138), calls=%async_computation.10 | async-start | bytes 9437184 | tf_op jit(solution)/shard_map/all_to_all | solution.py:219
  1011.5 58.8 %all-to-all-start.8 = ((bf16[8,4,73728]{2,0,1:T(8,128)(2,1)}), bf16[8,4,73728]{2,0,1:T(8,128)(2,1)}, u32[]{:S(2)}, u32[]{:S(2)}) async-start(bf16[8,4,73728]{2,0,1:T(8,128)(2,1)} %copy.135), calls=%async_computation.8 | async-start | bytes 9437184 | tf_op jit(solution)/shard_map/all_to_all | solution.py:219
  1022.1 54.6 %copy-start.91 = (f32[256]{0:T(256)S(1)}, f32[256]{0:T(256)}, u32[]{:S(2)}) copy-start(f32[256]{0:T(256)} %copy-done.90) | copy-start | bytes 3076
  1022.1 54.6 %copy-start.93 = (f32[256]{0:T(256)S(1)}, f32[256]{0:T(256)}, u32[]{:S(2)}) copy-start(f32[256]{0:T(256)} %copy-done.92) | copy-start | bytes 3076
  1022.1 54.6 %copy-start.95 = (f32[256]{0:T(256)S(1)}, f32[256]{0:T(256)}, u32[]{:S(2)}) copy-start(f32[256]{0:T(256)} %copy-done.94) | copy-start | bytes 3076
  1070.3 34.7 %all-to-all-start.11 = ((bf16[8,2,36864]{2,1,0:T(2,128)(2,1)}), bf16[8,2,36864]{2,1,0:T(2,128)(2,1)}, u32[]{:S(2)}, u32[]{:S(2)}) async-start(bf16[8,2,36864]{2,1,0:T(2,128)(2,1)} %reshape.1106), calls=%async_computation.11 | async-start | bytes 2359296 | tf_op jit(solution)/shard_map/all_to_all | solution.py:225
  1105.0 32.6 %all-to-all-start.9 = ((bf16[8,2,36864]{2,1,0:T(2,128)(2,1)}), bf16[8,2,36864]{2,1,0:T(2,128)(2,1)S(1)}, u32[]{:S(2)}, u32[]{:S(2)}) async-start(bf16[8,2,36864]{2,1,0:T(2,128)(2,1)} %reshape.1104), calls=%async_computation.9 | async-start | bytes 2359296 | tf_op jit(solution)/shard_map/all_to_all | solution.py:225
  (106 other events, 1134.9 us)
Sparse Core Ops, SparseCore 0:
  10.9 57.1 all-gather.18
  71.0 52.8 all-gather.14
  126.8 53.0 all-gather.16
  181.3 18.5 all-gather.28
  201.3 19.6 all-gather.26
  223.0 19.6 all-gather.30
  244.3 19.6 all-gather.32
  266.9 54.1 all-gather.20
  324.0 62.5 all-gather.22
  389.3 62.3 all-gather.24
where the time goes:
time: 1160 us; the launch traced here: 1150 us
  waiting for transfers between devices  572 us (49%)
  matrix products  164 us (14%)
  local copies, waits for them, and re-layouts  120 us (10%)
  starting transfers between devices  117 us (10%)
  other arithmetic  116 us (10%)
  blocking collectives  42.7 us (4%)
  between operations  16.4 us (1%)
    all_to_all x15, waiting for transfers between devices, owner_sum(): lax.all_to_all(as_sent(blocks), 'ctx', split_axis=1, concat_axis=1, tiled...  119 us
    ppermute x8, waiting for transfers between devices, shifted(): lax.ppermute(value, axis, [(i, (i + by) % peers) for i in range(peers)])  92.3 us
    all_to_all x15, waiting for transfers between devices, owner_sum(): lax.all_to_all(as_sent(partial_sums), 'dp', split_axis=0, concat_axis=0,...  67.2 us
    convert_element_type x40, local copies, waits for them, and re-layouts, as_sent(): a.astype(jnp.bfloat16)  63.7 us
    all_to_all x15, starting transfers between devices, owner_sum(): lax.all_to_all(as_sent(partial_sums), 'dp', split_axis=0, concat_axis=0,...  60 us
    all_gather x1, waiting for transfers between devices, on_device(): lax.all_gather(shards[5], ('dp', 'ctx'), axis=0, tiled=True)  56.5 us
    all_to_all x15, starting transfers between devices, owner_sum(): lax.all_to_all(as_sent(blocks), 'ctx', split_axis=1, concat_axis=1, tiled...  56.3 us
    all_gather x1, waiting for transfers between devices, on_device(): lax.all_gather(shards[2], ('dp', 'ctx'), axis=0, tiled=True)  53.2 us
  transfers between devices with their start and end apart: 48, of which 43 were waited for; matrix products, arithmetic and copies ran while one was open for 34% of the time, Pallas kernels for 0%

commit v1 on v0

--- a/solution.py
+++ b/solution.py
@@ -1,6 +1,7 @@
 import jax
 import jax.numpy as jnp
 from jax import lax
+from jax.sharding import Mesh
 from jax.sharding import PartitionSpec as P
 
 HEADS = 12
@@ -363,48 +364,355 @@
     )
 
 
+BF = jnp.bfloat16
+F32 = jnp.float32
+SMALL = 8
+
+
+def other_core(value):
+    return lax.ppermute(value, "core", [(0, 1), (1, 0)])
+
+
+def other_x(value):
+    return lax.ppermute(value, "x", [(0, 1), (1, 0)])
+
+
+def other_y(value):
+    return lax.ppermute(value, "y", [(0, 1), (1, 0)])
+
+
+def other_z(value, by):
+    return lax.ppermute(value, "z", [(i, i ^ by) for i in range(lax.axis_size("z"))])
+
+
+def pair(bit, own, received):
+    return jnp.stack((jnp.where(bit == 0, own, received), jnp.where(bit == 0, received, own)))
+
+
+def pick(value, index, axis):
+    return lax.dynamic_index_in_dim(value, index, axis, keepdims=False)
+
+
+def in_order(index, pieces):
+    level = list(pieces)
+    bit = 0
+    ordered = [p[None] for p in level]
+    while len(ordered) > 1:
+        flag = (index >> bit) & 1
+        ordered = [
+            jnp.concatenate(
+                (jnp.where(flag == 0, a, b), jnp.where(flag == 0, b, a)), axis=0
+            )
+            for a, b in zip(ordered[::2], ordered[1::2])
+        ]
+        bit += 1
+    return ordered[0]
+
+
+def gather_chips(unit, z, x, y):
+    z_count = lax.axis_size("z")
+    along_z = in_order(z, [unit] + [other_z(unit, k) for k in range(1, z_count)])
+    half = z_count // 2
+    first, second = along_z[:half], along_z[half:]
+    first = pair(x, first, other_x(first))
+    second = pair(y, second, other_y(second))
+    first = pair(y, first, other_y(first))
+    second = pair(x, second, other_x(second))
+    return jnp.concatenate((jnp.moveaxis(first, 2, 0).swapaxes(1, 2), jnp.moveaxis(second, 2, 0)))
+
+
+def reduce_chips(parts, z, x, y, y_first):
+    if y_first:
+        kept = pick(parts, y, 2).astype(F32) + other_y(pick(parts, 1 - y, 2).astype(BF)).astype(F32)
+        kept = pick(kept, x, 1) + other_x(pick(kept, 1 - x, 1).astype(BF)).astype(F32)
+    else:
+        kept = pick(parts, x, 1).astype(F32) + other_x(pick(parts, 1 - x, 1).astype(BF)).astype(F32)
+        kept = pick(kept, y, 1) + other_y(pick(kept, 1 - y, 1).astype(BF)).astype(F32)
+    total = pick(kept, z, 0)
+    for k in range(1, lax.axis_size("z")):
+        total = total + other_z(pick(kept, z ^ k, 0).astype(BF), k).astype(F32)
+    return total
+
+
+def mm(left, right, dims):
+    return lax.dot_general(left, right, (dims, ((), ())), preferred_element_type=F32)
+
+
+def norm_stats(values):
+    centre = values - jnp.mean(values, axis=-1, keepdims=True)
+    spread = jnp.mean(centre * centre, axis=-1, keepdims=True)
+    rate = lax.rsqrt(spread + 1e-05)
+    return centre * rate, rate
+
+
+def norm_back(unit, rate, gain, grad):
+    scaled = grad * gain
+    return rate * (
+        scaled
+        - jnp.mean(scaled, axis=-1, keepdims=True)
+        - unit * jnp.mean(scaled * unit, axis=-1, keepdims=True)
+    )
+
+
+def attend(queries, keys, values):
+    length, width = queries.shape
+    heads = width // DH
+    q, k, v = (a.reshape(length, heads, DH) for a in (queries, keys, values))
+    scores = jnp.einsum("qhd,khd->hqk", q, k, preferred_element_type=F32)
+    allowed = jnp.arange(length)[:, None] >= jnp.arange(length)[None, :]
+    scores = jnp.where(allowed, scores, -1e30)
+    row_max = jnp.max(scores, axis=-1, keepdims=True)
+    exp_scores = jnp.exp(scores - row_max)
+    row_total = jnp.sum(exp_scores, axis=-1, keepdims=True)
+    probs_low = (exp_scores / row_total).astype(BF)
+    mixed = jnp.einsum("hqk,khd->qhd", probs_low, v, preferred_element_type=F32)
+    return mixed.reshape(length, width).astype(BF), (row_max, row_total)
+
+
+def attend_back(queries, keys, values, kept, grad_mixed):
+    length, width = queries.shape
+    heads = width // DH
+    row_max, row_total = kept
+    q, k, v, g = (a.reshape(length, heads, DH) for a in (queries, keys, values, grad_mixed))
+    scores = jnp.einsum("qhd,khd->hqk", q, k, preferred_element_type=F32)
+    allowed = jnp.arange(length)[:, None] >= jnp.arange(length)[None, :]
+    scores = jnp.where(allowed, scores, -1e30)
+    probs = jnp.exp(scores - row_max) / row_total
+    probs_low = probs.astype(BF)
+    grad_probs = jnp.einsum("qhd,khd->hqk", g, v, preferred_element_type=F32)
+    inner = jnp.sum(probs * grad_probs, axis=-1, keepdims=True)
+    grad_scores = (probs * (grad_probs - inner)).astype(BF)
+    grad_q = jnp.einsum("hqk,khd->qhd", grad_scores, k, preferred_element_type=F32)
+    grad_k = jnp.einsum("hqk,qhd->khd", grad_scores, q, preferred_element_type=F32)
+    grad_v = jnp.einsum("hqk,qhd->khd", probs_low, g, preferred_element_type=F32)
+    return tuple(a.reshape(length, width).astype(BF) for a in (grad_q, grad_k, grad_v))
+
+
+def chip_step(
+    tokens_in,
+    out_grad,
+    w_query,
+    w_key,
+    w_value,
+    w_out,
+    w_up,
+    w_down,
+    b_query,
+    b_value,
+    b_out,
+    b_up,
+    b_down,
+    norm1_gain,
+    norm1_shift,
+    norm2_gain,
+    norm2_shift,
+):
+    z, x, y, core = (lax.axis_index(name) for name in ("z", "x", "y", "core"))
+    z_count = lax.axis_size("z")
+    chips = z_count * 4
+    half_chips = chips // 2
+    _, block, width = tokens_in.shape
+    half = width // 2
+    rows = w_query.shape[0]
+    hidden_rows = w_down.shape[0]
+    hidden = hidden_rows * chips
+    query_scale = DH ** (-0.5)
+
+    def own_positions(value):
+        return pair(y, pick(value, y, 0), other_y(pick(value, 1 - y, 0)))
+
+    def whole(mine):
+        return pair(core, mine, other_core(mine)).swapaxes(0, 1).reshape(4 * block, -1)
+
+    def own_rows(value, which):
+        return pick(value.reshape(2, 2, block, -1), which, 1)
+
+    def chip_sum(partial):
+        return own_rows(partial, core) + other_core(own_rows(partial, 1 - core).astype(BF)).astype(F32)
+
+    three = jnp.stack((w_query, w_key, w_value)).reshape(3, rows, 2, half)
+    vectors = (
+        b_query, b_value, b_out, b_down, norm1_gain, norm1_shift, norm2_gain, norm2_shift, b_up
+    )
+    small = jnp.concatenate(vectors)
+    small_rows = jnp.zeros((SMALL, half), BF).at[0, : small.shape[0]].set(small)
+    unit = pair(
+        core,
+        jnp.concatenate((pick(three, core, 2).reshape(3 * rows, half), small_rows)),
+        other_core(
+            jnp.concatenate((pick(three, 1 - core, 2).reshape(3 * rows, half), small_rows))
+        ),
+    )
+    up_parts = w_up.reshape(rows, chips, 2, hidden_rows)
+    up_unit = pair(
+        core,
+        pick(up_parts, core, 2).reshape(rows, hidden),
+        other_core(pick(up_parts, 1 - core, 2).reshape(rows, hidden)),
+    )
+    late = jnp.concatenate(
+        (up_unit.reshape(-1, width), w_down.reshape(-1, width), w_out.reshape(-1, width))
+    )
+    late = lax.all_gather(late, ("z", "x", "y"), axis=0, tiled=False)
+    mine = own_positions(tokens_in)
+    tokens = whole(mine).astype(F32)
+    mine32 = mine.astype(F32)
+    first = gather_chips(unit, z, x, y)
+    up_size = 2 * rows * hidden // width
+    up_c = late[:, :up_size].reshape(width, hidden)
+    down_c = late[:, up_size : up_size + hidden_rows].reshape(hidden, width)
+    out_parts = late[:, up_size + hidden_rows :].reshape(2, half_chips, rows, width)
+    out_c = (
+        pair(core, pick(out_parts, core, 0), other_core(pick(out_parts, 1 - core, 0)))
+        .swapaxes(0, 1)
+        .reshape(half, width)
+    )
+    three_c = first[..., : 3 * rows, :].reshape(chips * 2, 3, rows, half)
+    query_c, key_c, value_c = (three_c[:, i].reshape(width, half) for i in range(3))
+    small_all = first[..., 3 * rows, : small.shape[0]].reshape(chips * 2, -1)
+
+    def vector(i):
+        return small_all[:, i * rows : (i + 1) * rows].reshape(width).astype(F32)
+
+    def core_half(value):
+        return pick(value.reshape(2, half), core, 0)
+
+    bias_q, bias_v, bias_o, bias_d, gain1, shift1, gain2, shift2 = (vector(i) for i in range(8))
+    bias_u = pick(small_all[:, 8 * rows :].reshape(chips, 2, hidden_rows), core, 1)
+    bias_u = bias_u.reshape(hidden).astype(F32)
+
+    unit1, _ = norm_stats(tokens)
+    normed = (unit1 * gain1 + shift1).astype(BF)
+    rightwards = ((1,), (0,))
+    queries = ((mm(normed, query_c, rightwards) + core_half(bias_q)) * query_scale).astype(BF)
+    keys = mm(normed, key_c, rightwards).astype(BF)
+    values = (mm(normed, value_c, rightwards) + core_half(bias_v)).astype(BF)
+    mixed, kept = attend(queries, keys, values)
+    grad_mine = own_positions(out_grad)
+    grad_whole = whole(grad_mine)
+    residual = mine32 + chip_sum(mm(mixed, out_c, rightwards)) + bias_o
+    unit2, rate2 = norm_stats(residual)
+    normed2 = whole((unit2 * gain2 + shift2).astype(BF))
+    hidden_pre = mm(normed2, up_c, rightwards) + bias_u
+    active, gelu_pull = jax.vjp(gelu_tanh, hidden_pre)
+    active = active.astype(BF)
+    output = residual + chip_sum(mm(active, down_c, rightwards)) + bias_d
+    output = output.astype(BF)
+    layer_out = pair(y, pick(output, y, 0), other_y(pick(output, 1 - y, 0)))
+
+    across = ((1,), (1,))
+    over_rows = ((0,), (0,))
+    grad_pre32 = gelu_pull(mm(grad_whole, down_c, across))[0]
+    grad_pre = grad_pre32.astype(BF)
+    grad_normed2 = chip_sum(mm(grad_pre, up_c, across))
+    grad_residual = grad_mine.astype(F32) + norm_back(unit2, rate2, gain2, grad_normed2)
+    branch_mine = grad_residual.astype(BF)
+    branch = whole(branch_mine)
+    grad_up = mm(normed2, grad_pre, over_rows)
+    grad_down = mm(active, grad_whole, over_rows)
+    grad_out = mm(mixed, branch, over_rows).reshape(half_chips, 2, rows, width)
+    grad_out = pair(core, pick(grad_out, core, 1), other_core(pick(grad_out, 1 - core, 1).astype(BF)).astype(F32))
+    by_chip = (z_count, 2, 2)
+    sum_up = reduce_chips(grad_up.reshape(by_chip + (2 * rows, hidden)), z, x, y, True)
+    down_out = jnp.concatenate(
+        (grad_down.reshape(chips, hidden_rows, width), grad_out.reshape(chips, rows, width)), axis=1
+    )
+    sum_down_out = reduce_chips(down_out.reshape(by_chip + (-1, width)), z, x, y, False)
+    grad_mixed = mm(branch, out_c, across).astype(BF)
+    grad_q, grad_k, grad_v = attend_back(queries, keys, values, kept, grad_mixed)
+    grad_qkv = jnp.concatenate((grad_q * query_scale, grad_k, grad_v), axis=1)
+    weights_c = jnp.concatenate((query_c, key_c, value_c), axis=1)
+    grad_three = mm(normed, grad_qkv, over_rows)
+    grad_normed1 = chip_sum(mm(grad_qkv, weights_c, across))
+    unit1_mine, rate1_mine = norm_stats(mine32)
+    grad_tokens = grad_residual + norm_back(unit1_mine, rate1_mine, gain1, grad_normed1)
+    from_y = other_y(pick(grad_tokens, 1 - y, 0).astype(BF)).astype(F32)
+    grad_tokens = pair(y, pick(grad_tokens, y, 0), from_y)
+
+    def sums(value):
+        return jnp.sum(value.astype(F32), axis=tuple(range(value.ndim - 1)))
+
+    def placed(value):
+        return jnp.where(
+            (jnp.arange(2) == core)[:, None], value[None], jnp.zeros((), F32)
+        ).reshape(width)
+
+    bias_sums = sums(grad_qkv)
+    small_grads = [
+        placed(bias_sums[:half]),
+        placed(bias_sums[2 * half :]),
+        sums(branch_mine),
+        sums(grad_mine),
+        sums(grad_normed1 * unit1_mine),
+        sums(grad_normed1),
+        sums(grad_normed2 * unit2),
+        sums(grad_normed2),
+    ]
+    small_grads = [g.reshape(chips, 2, rows) for g in small_grads]
+    up_sums = sums(grad_pre).reshape(chips, 1, hidden_rows)
+    small_grads.append(
+        jnp.where((jnp.arange(2) == core)[None, :, None], up_sums, jnp.zeros((), F32))
+    )
+    small_grads = jnp.concatenate(small_grads, axis=2).reshape(chips, 1, -1)
+    last = grad_three.reshape(chips, 2 * rows, 3 * half)
+    last = jnp.concatenate(
+        (last, jnp.pad(small_grads, ((0, 0), (0, SMALL - 1), (0, 3 * half - small_grads.shape[2])))), axis=1
+    )
+    last_a = reduce_chips(last[:, :, : 3 * half // 2].reshape(by_chip + (-1, 3 * half // 2)), z, x, y, True)
+    last_b = reduce_chips(last[:, :, 3 * half // 2 :].reshape(by_chip + (-1, 3 * half // 2)), z, x, y, False)
+    last = jnp.concatenate((last_a, last_b), axis=1)
+    small_mine = last[2 * rows, : 2 * small.shape[0]].reshape(2, -1)
+    small_sum = pick(small_mine, core, 0) + other_core(pick(small_mine, 1 - core, 0))
+    three_mine = last[: 2 * rows].reshape(2, rows, 3 * half)
+    up_mine = sum_up.reshape(2, rows, hidden)
+    to_core = jnp.concatenate((pick(three_mine, 1 - core, 0), pick(up_mine, 1 - core, 0)), axis=1)
+    to_core = other_core(to_core)
+    three_out = pair(core, pick(three_mine, core, 0), to_core[:, : 3 * half])
+    three_out = three_out.reshape(2, rows, 3, half)
+    up_out = pair(core, pick(up_mine, core, 0), to_core[:, 3 * half :])
+    up_out = up_out.reshape(2, rows, chips, hidden_rows)
+    up_out = jnp.moveaxis(up_out, 0, 2).reshape(rows, 2 * hidden)
+    three_out = jnp.moveaxis(three_out, 0, 2)
+    g_q, g_k, g_v = (three_out[:, i].reshape(rows, width) for i in range(3))
+    g_small = [small_sum[i * rows : (i + 1) * rows] for i in range(8)]
+    return (
+        layer_out,
+        grad_tokens,
+        g_q,
+        g_k,
+        g_v,
+        sum_down_out[hidden_rows:],
+        up_out,
+        sum_down_out[:hidden_rows],
+        g_small[0],
+        g_small[1],
+        g_small[2],
+        small_sum[8 * rows :],
+        g_small[3],
+        g_small[4],
+        g_small[5],
+        g_small[6],
+        g_small[7],
+    )
+
+
 def solution(mesh):
-    placed = (
-        P("dp", "ctx", None),
-        P("dp", "ctx", None),
-        P(("dp", "ctx"), None),
-        P(("dp", "ctx"), None),
-        P(("dp", "ctx"), None),
-        P(("dp", "ctx"), None),
-        P(("dp", "ctx"), None),
-        P(("dp", "ctx"), None),
-        P(("dp", "ctx")),
-        P(("dp", "ctx")),
-        P(("dp", "ctx")),
-        P(("dp", "ctx")),
-        P(("dp", "ctx")),
-        P(("dp", "ctx")),
-        P(("dp", "ctx")),
-        P(("dp", "ctx")),
-        P(("dp", "ctx")),
-    )
-    return jax.shard_map(
-        on_device,
-        mesh=mesh,
-        in_specs=placed,
-        out_specs=(
-            P("dp", "ctx", None),
-            P("dp", "ctx", None),
-            P(("dp", "ctx"), None),
-            P(("dp", "ctx"), None),
-            P(("dp", "ctx"), None),
-            P(("dp", "ctx"), None),
-            P(("dp", "ctx"), None),
-            P(("dp", "ctx"), None),
-            P(("dp", "ctx")),
-            P(("dp", "ctx")),
-            P(("dp", "ctx")),
-            P(("dp", "ctx")),
-            P(("dp", "ctx")),
-            P(("dp", "ctx")),
-            P(("dp", "ctx")),
-            P(("dp", "ctx")),
-            P(("dp", "ctx")),
-        ),
-        check_vma=False,
-    )
+    dp_count, ctx_count = mesh.shape["dp"], mesh.shape["ctx"]
+
+    def run(*args):
+        per_dp = args[0].shape[0] // dp_count
+        if ctx_count == 4 and per_dp == 2 and dp_count == 8:
+            devices = mesh.devices.reshape(dp_count // 2, 2, ctx_count // 2, 2)
+            used = Mesh(devices, ("z", "x", "y", "core"))
+            body, dp, ctx = chip_step, ("z", "x"), ("y", "core")
+        else:
+            used, body, dp, ctx = mesh, on_device, ("dp",), ("ctx",)
+        tokens, matrix, bias = P(dp, ctx, None), P(dp + ctx, None), P(dp + ctx)
+        return jax.shard_map(
+            body,
+            mesh=used,
+            in_specs=(tokens,) * 2 + (matrix,) * 6 + (bias,) * 9,
+            out_specs=(tokens,) * 2 + (matrix,) * 6 + (bias,) * 9,
+            check_vma=False,
+        )(*args)
+
+    return run

time: 1160 us -> 469 us (0.40)
  waiting for transfers between devices: 572 us -> 145 us
  starting transfers between devices: 117 us -> 46.6 us
  other arithmetic: 116 us -> 60.9 us
  local copies, waits for them, and re-layouts: 120 us -> 67.2 us
  blocking collectives: 42.7 us -> 0 us
  matrix products: 164 us -> 124 us
    all_gather x10 -> x1, waiting for transfers between devices: 290 us -> 16.4 us  [chip_step(): late = lax.all_gather(late, ('z', 'x', 'y'), axis=0, tiled=False)]
    all_to_all x30 -> x0, waiting for transfers between devices: 186 us -> none  [the longest x15 119 us: owner_sum(): lax.all_to_all(as_sent(blocks), 'ctx', split_axis=1, concat_axis=1, tiled...]
    all_to_all x30 -> x0, starting transfers between devices: 116 us -> none  [the longest x15 60 us: owner_sum(): lax.all_to_all(as_sent(partial_sums), 'dp', split_axis=0, concat_axis=0,...]
    convert_element_type x44 -> x32, local copies, waits for them, and re-layouts: 68.9 us -> 17.5 us  [the longest x1 4.65 us: chip_step(): active = active.astype(BF)]
    ppermute x8 -> x45, starting transfers between devices: 0.5 us -> 46.6 us  [the longest x15 20.4 us: other_z(): lax.ppermute(value, 'z', [(i, i ^ by) for i in range(lax.axis_size('z'))])]
    unnamed x1 -> x0, blocking collectives: 42.7 us -> none
    convert_element_type x42 -> x8, other arithmetic: 64.1 us -> 22.4 us  [the longest x1 17.2 us: attend_back(): grad_scores = (probs * (grad_probs - inner)).astype(BF)]
    ppermute x8 -> x45, waiting for transfers between devices: 92.3 us -> 129 us  [the longest x10 68.4 us: other_y(): return lax.ppermute(value, 'y', [(0, 1), (1, 0)])]
  transfers between devices with their start and end apart: 48 -> 46, of which waited for: 43 -> 22; matrix products, arithmetic and copies ran while one was open for 34% -> 43% of each run, Pallas kernels for 0% -> 0%
where the time goes in v1:
time: 469 us; the launch traced here: 460 us
  waiting for transfers between devices  145 us (31%)
  matrix products  124 us (26%)
  local copies, waits for them, and re-layouts  67.2 us (14%)
  other arithmetic  60.9 us (13%)
  starting transfers between devices  46.6 us (10%)
  between operations  16.1 us (3%)
    ppermute x10, waiting for transfers between devices, other_y(): return lax.ppermute(value, 'y', [(0, 1), (1, 0)])  68.4 us
    dot_general x14, matrix products, mm(): lax.dot_general(left, right, (dims, ((), ())), preferred_element_type=F32)  56.2 us
    ppermute x15, waiting for transfers between devices, other_z(): lax.ppermute(value, 'z', [(i, i ^ by) for i in range(lax.axis_size('z'))])  46.3 us
    ppermute x15, starting transfers between devices, other_z(): lax.ppermute(value, 'z', [(i, i ^ by) for i in range(lax.axis_size('z'))])  20.4 us
    dot_general x1, matrix products, attend_back(): grad_probs = jnp.einsum('qhd,khd->hqk', g, v, preferred_element_type=F32)  17.2 us
    convert_element_type x1, other arithmetic, attend_back(): grad_scores = (probs * (grad_probs - inner)).astype(BF)  17.2 us
    all_gather x1, waiting for transfers between devices, chip_step(): late = lax.all_gather(late, ('z', 'x', 'y'), axis=0, tiled=False)  16.4 us
    sub x1, matrix products, attend(): exp_scores = jnp.exp(scores - row_max)  15.8 us
  transfers between devices with their start and end apart: 46, of which 22 were waited for; matrix products, arithmetic and copies ran while one was open for 43% of the time, Pallas kernels for 0%

profile of v1, /device:TPU:0, one launch (start us, length us, event | category | flops | bytes accessed | tf_op | source)
XLA Modules:
  0.0 460.3 jit_solution(16794153432850120198)
XLA Ops:
  15.1 2.7 collective-permute-start.16
  18.7 2.1 collective-permute-start.3
  22.1 2.5 collective-permute-start.5
  24.8 6.2 %collective-permute-done.5 = bf16[2,80,384]{2,1,0:T(8,128)(2,1)S(1)} collective-permute-done((bf16[2,80,384]{2,1,0:T(8,128)(2,1)S(1)}, bf16[2,80,384]{2,1,0:T(8,128)(2,1)S(1)}, u32[]{:S(2)}, u32[]{:S(2)}) %collective-permute-start.5) | collective-permute-done | bytes 122912 | tf_op jit(solution)/shard_map/ppermute | solution.py:385
  31.0 11.6 %collective-permute-done.4 = bf16[2,80,384]{2,1,0:T(8,128)(2,1)S(1)} collective-permute-done((bf16[2,80,384]{2,1,0:T(8,128)(2,1)S(1)}, bf16[2,80,384]{2,1,0:T(8,128)(2,1)S(1)}, u32[]{:S(2)}, u32[]{:S(2)}) %collective-permute-start.4) | collective-permute-done | bytes 122912 | tf_op jit(solution)/shard_map/ppermute | solution.py:385
  53.3 13.0 %collective-permute-done.7 = bf16[2,2,2,80,384]{4,3,2,1,0:T(8,128)(2,1)S(1)} collective-permute-done((bf16[2,2,2,80,384]{4,3,2,1,0:T(8,128)(2,1)S(1)}, bf16[2,2,2,80,384]{4,3,2,1,0:T(8,128)(2,1)S(1)}, u32[]{:S(2)}, u32[]{:S(2)}) %collective-permute-start.7) | collective-permute-done | bytes 491552 | tf_op jit(solution)/shard_map/ppermute | solution.py:381
  66.6 4.5 collective-permute-done.9
  75.2 1.8 select_bitcast_fusion.7
  78.7 1.7 convolution_convert_fusion.1
  80.5 1.7 multiply_convert_fusion.2
  82.2 1.7 add_convert_fusion.2
  83.9 15.8 %fusion.137 = (f32[6,1024]{1,0:T(8,128)}, f32[6,1024,1024]{1,2,0:T(8,128)}) fusion(pred[1024,1024]{0,1:T(8,128)(4,1)S(1)} %copy-done.37, bf16[1024,6,64]{0,2,1:T(8,128)(2,1)} %bitcast.468, bf16[1024,6,64]{0,2,1:T(8,128)(2,1)} %bitcast.466), kind=kOutput, calls=%fused_computation.325 | convolution fusion | flops 824181760 | bytes 27811840 | tf_op jit(solution)/shard_map/sub | solution.py:465
  99.8 16.4 %all-gather.3.cloned.1.call-done = bf16[3456,768]{1,0:T(8,128)(2,1)} async-done(((bf16[216,768]{1,0:T(8,128)(2,1)}), bf16[3456,768]{1,0:T(8,128)(2,1)}) %all-gather.3.cloned.1.call-update) | async-done | bytes 5308432 | tf_op jit(solution)/shard_map/all_gather | solution.py:555
  117.4 11.6 %fusion.59 = bf16[6,64,1024]{2,1,0:T(8,128)(2,1)} fusion(bf16[1024,6,64]{0,2,1:T(8,128)(2,1)} %bitcast.494, f32[6,1024,1024]{1,2,0:T(8,128)} %get-tuple-element.140, f32[6,1024]{1,0:T(8,128)} %get-tuple-element.139), kind=kOutput, calls=%fused_computation.116 | convolution fusion | flops 818282496 | bytes 26763264 | tf_op jit(solution)/shard_map/hqk,khd->qhd/dot_general | solution.py:468
  129.0 3.1 convert_element_type.460
  137.7 1.7 fusion.26
  140.3 1.8 fusion.129
  146.9 2.6 copy.136
  149.5 4.9 %fusion.131 = (bf16[16,96,768]{2,1,0:T(8,128)(2,1)}, bf16[16,96,768]{2,1,0:T(8,128)(2,1)}) fusion(bf16[16,216,768]{2,1,0:T(8,128)(2,1)} %bitcast.441), kind=kLoop, calls=%fused_computation.319 | loop fusion | bytes 9437184 | tf_op jit(solution)/shard_map/slice | solution.py:562
  154.3 4.8 %reshape.542 = bf16[768,1536,1,1]{1,0,2,3:T(8,128)(2,1)} reshape(bf16[16,96,768]{2,1,0:T(8,128)(2,1)} %get-tuple-element.51) | data formatting | bytes 4718592 | tf_op jit(solution)/shard_map/reshape | solution.py:561
  159.1 4.7 %reshape.510 = bf16[768,1536]{1,0:T(8,128)(2,1)} reshape(bf16[16,96,768]{2,1,0:T(8,128)(2,1)} %get-tuple-element.51) | data formatting | bytes 4718592 | tf_op jit(solution)/shard_map/reshape | solution.py:561
  167.4 2.6 copy.139
  170.1 9.3 %fusion.16 = (bf16[1536,1024]{0,1:T(8,128)(2,1)}, f32[1024,1536]{1,0:T(8,128)}) fusion(f32[1536]{0:T(1024)S(1)} %copy-done.60, bf16[1024,768]{1,0:T(8,128)(2,1)} %bitcast.438, bf16[768,1536]{1,0:T(8,128)(2,1)} %reshape.510), kind=kOutput, calls=%fused_computation.26 | convolution fusion | flops 2431647744 | bytes 13375488 | tf_op jit(solution)/shard_map/dot_general | solution.py:438
  179.4 4.7 %copy.143 = bf16[1536,1024]{1,0:T(8,128)(2,1)} copy(bf16[1536,1024]{0,1:T(8,128)(2,1)} %get-tuple-element.143) | data formatting | bytes 6291456 | tf_op jit(solution)/shard_map/convert_element_type | solution.py:597
  184.0 12.2 %convert_reduce_fusion = (f32[1536]{0:T(1024)S(1)}, bf16[1024,1536]{1,0:T(8,128)(2,1)}, bf16[1024,1536]{1,0:T(8,128)(2,1)}) fusion(f32[1024,1536]{1,0:T(8,128)} %get-tuple-element.144, f32[1536]{0:T(1024)S(1)} %copy-done.60, bf16[1024,768]{1,0:T(8,128)(2,1)} %bitcast.454, bf16[1536,768]{1,0:T(8,128)(2,1)} %bitcast.449), kind=kOutput, calls=%fused_computation.28 | convolution fusion | flops 2461530624 | bytes 16527360 | tf_op jit(solution)/shard_map/dot_general | solution.py:438
  196.3 5.4 %fusion.35 = f32[2,2,256,768]{3,2,1,0:T(8,128)S(1)} fusion(bf16[2,2,256,1536]{3,2,1,0:T(8,128)(2,1)} %bitcast.492, bf16[768,1536,1,1]{1,0,2,3:T(8,128)(2,1)} %reshape.542), kind=kOutput, calls=%fused_computation.63 | convolution fusion | flops 2415919104 | bytes 8650752 | tf_op jit(solution)/shard_map/dot_general | solution.py:438
  201.8 2.6 fusion.138
  205.1 2.6 fusion.21
  210.4 4.2 fusion.139
  215.5 2.0 convert_reduce_fusion.4
  219.4 18.6 %collective-permute-done.32 = bf16[4,2,48,1536]{3,2,1,0:T(8,128)(2,1)} collective-permute-done((bf16[4,2,48,1536]{3,2,1,0:T(8,128)(2,1)}, bf16[4,2,48,1536]{3,2,1,0:T(8,128)(2,1)}, u32[]{:S(2)}, u32[]{:S(2)}) %collective-permute-start.32) | collective-permute-done | bytes 1179680 | tf_op jit(solution)/shard_map/ppermute | solution.py:381
  238.0 2.3 bitcast_add_fusion
  242.7 2.7 collective-permute-done.15
  247.9 1.7 convolution_convert_fusion
  249.6 13.3 %fusion.62 = bf16[6,64,1024]{2,1,0:T(8,128)(2,1)} fusion(bf16[1024,6,64]{0,2,1:T(8,128)(2,1)} %bitcast.496, f32[6,1024,1024]{1,2,0:T(8,128)} %get-tuple-element.140, f32[6,1024]{1,0:T(8,128)S(1)} %copy-done.56), kind=kOutput, calls=%fused_computation.117 | convolution fusion | flops 818282496 | bytes 26763264 | tf_op jit(solution)/shard_map/hqk,qhd->khd/dot_general | solution.py:487
  262.9 17.2 %multiply_reduce_fusion = (f32[6,1024]{1,0:T(8,128)}, f32[6,1024,1024]{1,2,0:T(8,128)}) fusion(f32[6,1024,1024]{1,2,0:T(8,128)} %get-tuple-element.140, f32[6,1024]{1,0:T(8,128)S(1)} %copy-done.56, bf16[1024,6,64]{0,2,1:T(8,128)(2,1)} %bitcast.497, bf16[1024,6,64]{0,2,1:T(8,128)(2,1)S(1)} %bitcast.495), kind=kOutput, calls=%fused_computation.2 | convolution fusion | flops 824174592 | bytes 51953664 | tf_op jit(solution)/shard_map/qhd,khd->hqk/dot_general | solution.py:482
  280.1 17.2 %multiply_convert_fusion = bf16[6,1024,1024]{1,2,0:T(8,128)(2,1)S(1)} fusion(f32[6,1024,1024]{1,2,0:T(8,128)} %get-tuple-element.142, f32[6,1024]{1,0:T(8,128)} %get-tuple-element.141, f32[6,1024,1024]{1,2,0:T(8,128)} %get-tuple-element.140, f32[6,1024]{1,0:T(8,128)} %get-tuple-element.139), kind=kLoop, calls=%fused_computation.1 | loop fusion | flops 25165824 | bytes 62963712 | tf_op jit(solution)/shard_map/convert_element_type | solution.py:484
  297.3 6.0 %convolution_convert_fusion.2 = bf16[6,64,1024]{2,1,0:T(8,128)(2,1)} fusion(bf16[1024,6,64]{0,2,1:T(8,128)(2,1)} %bitcast.469, bf16[6,1024,1024]{1,2,0:T(8,128)(2,1)S(1)} %multiply_convert_fusion), kind=kOutput, calls=%fused_computation.118 | convolution fusion | flops 805699584 | bytes 14155776 | tf_op jit(solution)/shard_map/hqk,qhd->khd/dot_general | solution.py:486
  303.2 4.3 fusion.65
  307.5 2.4 copy.131
  309.9 2.4 copy.129
  313.6 2.1 convert_reduce_fusion.1
  315.8 5.3 %fusion.42 = f32[1024,768]{1,0:T(8,128)} fusion(bf16[768,384]{1,0:T(8,128)(2,1)} %bitcast.478, bf16[768,384]{1,0:T(8,128)(2,1)S(1)} %bitcast.474, bf16[768,384]{1,0:T(8,128)(2,1)S(1)} %bitcast.476, bf16[1024,384]{1,0:T(8,128)(2,1)} %copy.131, bf16[1024,384]{1,0:T(8,128)(2,1)S(1)} %copy-done.23, bf16[1024,384]{1,0:T(8,128)(2,1)S(1)} %copy-done.22), kind=kOutput, calls=%fused_computation.74 | convolution fusion | flops 1824325632 | bytes 7274496 | tf_op jit(solution)/shard_map/dot_general | solution.py:438
  325.5 6.0 %fusion.33 = f32[16,48,1152]{2,1,0:T(8,128)} fusion(bf16[16,48,1024]{2,1,0:T(8,128)(2,1)} %bitcast.453, bf16[1024,384]{1,0:T(8,128)(2,1)S(1)} %copy-done.21, bf16[1024,384]{1,0:T(8,128)(2,1)} %copy.130, bf16[1024,384]{1,0:T(8,128)(2,1)} %copy.129), kind=kOutput, calls=%fused_computation.61 | convolution fusion | flops 1819017216 | bytes 7471104 | tf_op jit(solution)/shard_map/dot_general | solution.py:438
  334.2 2.0 collective-permute-start.36
  339.6 4.5 collective-permute-done.36
  344.1 5.2 %collective-permute-done.35 = bf16[48,1536]{1,0:T(8,128)(2,1)S(1)} collective-permute-done((bf16[48,1536]{1,0:T(8,128)(2,1)S(1)}, bf16[48,1536]{1,0:T(8,128)(2,1)S(1)}, u32[]{:S(2)}, u32[]{:S(2)}) %collective-permute-start.35) | collective-permute-done | bytes 147488 | tf_op jit(solution)/shard_map/ppermute | solution.py:385
  350.8 1.9 fusion.52
  353.4 2.9 fusion.51
  361.2 7.3 %collective-permute-done.21 = bf16[256,768]{1,0:T(8,128)(2,1)S(1)} collective-permute-done((bf16[256,768]{1,0:T(8,128)(2,1)S(1)}, bf16[256,768]{1,0:T(8,128)(2,1)S(1)}, u32[]{:S(2)}, u32[]{:S(2)}) %collective-permute-start.21) | collective-permute-done | bytes 393248 | tf_op jit(solution)/shard_map/ppermute | solution.py:381
  369.8 9.3 %collective-permute-done.22 = bf16[4,2,56,576]{3,2,0,1:T(8,128)(2,1)S(1)} collective-permute-done((bf16[4,2,56,576]{3,2,0,1:T(8,128)(2,1)S(1)}, bf16[4,2,56,576]{3,2,0,1:T(8,128)(2,1)S(1)}, u32[]{:S(2)}, u32[]{:S(2)}) %collective-permute-start.22) | collective-permute-done | bytes 516128 | tf_op jit(solution)/shard_map/ppermute | solution.py:381
  380.7 5.2 %collective-permute-done.27 = bf16[4,2,56,576]{3,2,1,0:T(8,128)(2,1)S(1)} collective-permute-done((bf16[4,2,56,576]{3,2,1,0:T(8,128)(2,1)S(1)}, bf16[4,2,56,576]{3,2,1,0:T(8,128)(2,1)S(1)}, u32[]{:S(2)}, u32[]{:S(2)}) %collective-permute-start.27) | collective-permute-done | bytes 516128 | tf_op jit(solution)/shard_map/ppermute | solution.py:377
  387.6 2.7 collective-permute-done.23
  390.4 2.1 collective-permute-start.24
  392.5 2.0 collective-permute-start.26
  394.7 2.4 collective-permute-start.29
  397.1 2.0 collective-permute-start.31
  399.1 5.1 %collective-permute-done.25 = bf16[56,576]{1,0:T(8,128)(2,1)S(1)} collective-permute-done((bf16[56,576]{1,0:T(8,128)(2,1)S(1)}, bf16[56,576]{1,0:T(8,128)(2,1)S(1)}, u32[]{:S(2)}, u32[]{:S(2)}) %collective-permute-start.25) | collective-permute-done | bytes 64544 | tf_op jit(solution)/shard_map/ppermute | solution.py:385
  404.5 1.9 collective-permute-done.30
  407.9 2.4 fusion.31
  413.8 17.1 %collective-permute-done.40 = bf16[4,120,768]{2,1,0:T(8,128)(2,1)S(1)} collective-permute-done((bf16[4,120,768]{2,1,0:T(8,128)(2,1)S(1)}, bf16[4,120,768]{2,1,0:T(8,128)(2,1)S(1)}, u32[]{:S(2)}, u32[]{:S(2)}) %collective-permute-start.40) | collective-permute-done | bytes 737312 | tf_op jit(solution)/shard_map/ppermute | solution.py:381
  432.6 2.1 collective-permute-start.43
  440.3 3.8 collective-permute-done.43
  444.1 7.7 %collective-permute-done.42 = bf16[120,768]{1,0:T(8,128)(2,1)S(1)} collective-permute-done((bf16[120,768]{1,0:T(8,128)(2,1)S(1)}, bf16[120,768]{1,0:T(8,128)(2,1)S(1)}, u32[]{:S(2)}, u32[]{:S(2)}) %collective-permute-start.42) | collective-permute-done | bytes 184352 | tf_op jit(solution)/shard_map/ppermute | solution.py:385
  (402 shorter events, 90.4 us)
Async XLA Ops:
  7.3 7.0 %copy-start.39 = (bf16[2,256,768]{2,1,0:T(8,128)(2,1)S(1)}, bf16[2,256,768]{2,1,0:T(8,128)(2,1)}, u32[]{:S(2)}) copy-start(bf16[2,256,768]{2,1,0:T(8,128)(2,1)} %param.20) | copy-start | bytes 2359300
  7.3 108.8 %all-gather.3.cloned.1.call-start = ((), (), s32[]{:S(2)}) async-start(), calls=%async_computation | async-start | bytes 5640192 | tf_op jit(solution)/shard_map/all_gather | solution.py:555
  8.7 9.1 %copy-start.40 = (bf16[2,256,768]{2,1,0:T(8,128)(2,1)S(1)}, bf16[2,256,768]{2,1,0:T(8,128)(2,1)}, u32[]{:S(2)}) copy-start(bf16[2,256,768]{2,1,0:T(8,128)(2,1)} %param.19) | copy-start | bytes 2359300
  10.1 1.4 collective-permute-start.10
  13.9 4.7 %collective-permute-start.2 = (bf16[80,384]{1,0:T(8,128)(2,1)S(1)}, bf16[80,384]{1,0:T(8,128)(2,1)S(1)}, u32[]{:S(2)}, u32[]{:S(2)}) collective-permute-start(bf16[80,384]{1,0:T(8,128)(2,1)S(1)} %fusion.115), channel_id=1, source_target_pairs={{0,1},{1,0},{2,3},{3,2},{4,5},{5,4},{6,7},{7,6},{8,9},{9,8},{10,11... | collective-permute-start | bytes 184328 | tf_op jit(solution)/shard_map/ppermute | solution.py:373
  15.1 30.7 %collective-permute-start.16 = (bf16[256,768]{1,0:T(8,128)(2,1)}, bf16[256,768]{1,0:T(8,128)(2,1)}, u32[]{:S(2)}, u32[]{:S(2)}) collective-permute-start(bf16[256,768]{1,0:T(8,128)(2,1)} %dynamic-slice_bitcast_fusion), channel_id=1, source_target_pairs={{0,2},{2,0},{1,3},{3,1},{4,6},{6,4},{5,7},{7,5},{8,10},{10,8},{9,1... | collective-permute-start | bytes 1179656 | tf_op jit(solution)/shard_map/ppermute | solution.py:381
  17.8 30.2 %collective-permute-start = (bf16[256,768]{1,0:T(8,128)(2,1)S(1)}, bf16[256,768]{1,0:T(8,128)(2,1)S(1)}, u32[]{:S(2)}, u32[]{:S(2)}) collective-permute-start(bf16[256,768]{1,0:T(8,128)(2,1)S(1)} %dynamic-slice_bitcast_fusion.2), channel_id=1, source_target_pairs={{0,2},{2,0},{1,3},{3,1},{4,6},{6,4},{5,7},{7,5},{8,10},{10,8},{9,1... | collective-permute-start | bytes 1179656 | tf_op jit(solution)/shard_map/ppermute | solution.py:381
  18.7 6.0 %collective-permute-start.3 = (bf16[2,80,384]{2,1,0:T(8,128)(2,1)S(1)}, bf16[2,80,384]{2,1,0:T(8,128)(2,1)S(1)}, u32[]{:S(2)}, u32[]{:S(2)}) collective-permute-start(bf16[2,80,384]{2,1,0:T(8,128)(2,1)S(1)} %pad_maximum_fusion.16), channel_id=1, source_target_pairs={{0,8},{8,0},{16,24},{24,16},{1,9},{9,1},{17,25},{25,17},{2,10},{10... | collective-permute-start | bytes 368648 | tf_op jit(solution)/shard_map/ppermute | solution.py:385
  22.1 8.9 %collective-permute-start.5 = (bf16[2,80,384]{2,1,0:T(8,128)(2,1)S(1)}, bf16[2,80,384]{2,1,0:T(8,128)(2,1)S(1)}, u32[]{:S(2)}, u32[]{:S(2)}) collective-permute-start(bf16[2,80,384]{2,1,0:T(8,128)(2,1)S(1)} %pad_maximum_fusion.16), channel_id=1, source_target_pairs={{0,24},{8,16},{16,8},{24,0},{1,25},{9,17},{17,9},{25,1},{2,26},{10... | collective-permute-start | bytes 368648 | tf_op jit(solution)/shard_map/ppermute | solution.py:385
  24.6 18.0 %collective-permute-start.4 = (bf16[2,80,384]{2,1,0:T(8,128)(2,1)S(1)}, bf16[2,80,384]{2,1,0:T(8,128)(2,1)S(1)}, u32[]{:S(2)}, u32[]{:S(2)}) collective-permute-start(bf16[2,80,384]{2,1,0:T(8,128)(2,1)S(1)} %pad_maximum_fusion.16), channel_id=1, source_target_pairs={{0,16},{8,24},{16,0},{24,8},{1,17},{9,25},{17,1},{25,9},{2,18},{10... | collective-permute-start | bytes 368648 | tf_op jit(solution)/shard_map/ppermute | solution.py:385
  24.7 23.3 %copy-start.41 = (bf16[2,256,768]{2,1,0:T(8,128)(2,1)S(1)}, bf16[2,256,768]{2,1,0:T(8,128)(2,1)}, u32[]{:S(2)}) copy-start(bf16[2,256,768]{2,1,0:T(8,128)(2,1)} %param.19) | copy-start | bytes 2359300
  42.7 6.3 %collective-permute-start.6 = (bf16[2,2,80,384]{3,2,1,0:T(8,128)(2,1)S(1)}, bf16[2,2,80,384]{3,2,1,0:T(8,128)(2,1)S(1)}, u32[]{:S(2)}, u32[]{:S(2)}) collective-permute-start(bf16[2,2,80,384]{3,2,1,0:T(8,128)(2,1)S(1)} %get-tuple-element.100), channel_id=1, source_target_pairs={{0,4},{4,0},{1,5},{5,1},{2,6},{6,2},{3,7},{7,3},{8,12},{12,8},{9,1... | collective-permute-start | bytes 737288 | tf_op jit(solution)/shard_map/ppermute | solution.py:377
  44.2 6.8 %collective-permute-start.8 = (bf16[2,2,80,384]{3,2,1,0:T(8,128)(2,1)S(1)}, bf16[2,2,80,384]{3,2,1,0:T(8,128)(2,1)S(1)}, u32[]{:S(2)}, u32[]{:S(2)}) collective-permute-start(bf16[2,2,80,384]{3,2,1,0:T(8,128)(2,1)S(1)} %get-tuple-element.101), channel_id=1, source_target_pairs={{0,2},{2,0},{1,3},{3,1},{4,6},{6,4},{5,7},{7,5},{8,10},{10,8},{9,1... | collective-permute-start | bytes 737288 | tf_op jit(solution)/shard_map/ppermute | solution.py:381
  48.0 96.2 %collective-permute-start.17 = (bf16[2,256,768]{2,1,0:T(8,128)(2,1)}, bf16[2,256,768]{2,1,0:T(8,128)(2,1)}, u32[]{:S(2)}, u32[]{:S(2)}) collective-permute-start(bf16[2,256,768]{2,1,0:T(8,128)(2,1)} %pad_maximum_fusion.7), channel_id=1, source_target_pairs={{0,1},{1,0},{2,3},{3,2},{4,5},{5,4},{6,7},{7,6},{8,9},{9,8},{10,11... | collective-permute-start | bytes 2359304 | tf_op jit(solution)/shard_map/ppermute | solution.py:373
  48.1 86.9 %copy-start.2 = (bf16[1,256,768]{2,1,0:T(8,128)(2,1)}, bf16[1,256,768]{2,1,0:T(8,128)(2,1)S(1)}, u32[]{:S(2)}) copy-start(bf16[1,256,768]{2,1,0:T(8,128)(2,1)S(1)} %get-tuple-element.81) | copy-start | bytes 1179652
  48.1 91.3 %copy-start = (bf16[1,256,768]{2,1,0:T(8,128)(2,1)}, bf16[1,256,768]{2,1,0:T(8,128)(2,1)S(1)}, u32[]{:S(2)}) copy-start(bf16[1,256,768]{2,1,0:T(8,128)(2,1)S(1)} %get-tuple-element.80) | copy-start | bytes 1179652
  49.1 17.3 %collective-permute-start.7 = (bf16[2,2,2,80,384]{4,3,2,1,0:T(8,128)(2,1)S(1)}, bf16[2,2,2,80,384]{4,3,2,1,0:T(8,128)(2,1)S(1)}, u32[]{:S(2)}, u32[]{:S(2)}) collective-permute-start(bf16[2,2,2,80,384]{4,3,2,1,0:T(8,128)(2,1)S(1)} %pad_maximum_fusion.8), channel_id=1, source_target_pairs={{0,2},{2,0},{1,3},{3,1},{4,6},{6,4},{5,7},{7,5},{8,10},{10,8},{9,1... | collective-permute-start | bytes 1474568 | tf_op jit(solution)/shard_map/ppermute | solution.py:381
  51.1 20.0 %collective-permute-start.9 = (bf16[2,2,2,80,384]{4,3,2,1,0:T(8,128)(2,1)S(1)}, bf16[2,2,2,80,384]{4,3,2,1,0:T(8,128)(2,1)S(1)}, u32[]{:S(2)}, u32[]{:S(2)}) collective-permute-start(bf16[2,2,2,80,384]{4,3,2,1,0:T(8,128)(2,1)S(1)} %pad_maximum_fusion.9), channel_id=1, source_target_pairs={{0,4},{4,0},{1,5},{5,1},{2,6},{6,2},{3,7},{7,3},{8,12},{12,8},{9,1... | collective-permute-start | bytes 1474568 | tf_op jit(solution)/shard_map/ppermute | solution.py:377
  53.3 21.9 %collective-permute-start.1 = (bf16[2,256,768]{2,1,0:T(8,128)(2,1)}, bf16[2,256,768]{2,1,0:T(8,128)(2,1)}, u32[]{:S(2)}, u32[]{:S(2)}) collective-permute-start(bf16[2,256,768]{2,1,0:T(8,128)(2,1)} %pad_maximum_fusion.5), channel_id=1, source_target_pairs={{0,1},{1,0},{2,3},{3,2},{4,5},{5,4},{6,7},{7,6},{8,9},{9,8},{10,11... | collective-permute-start | bytes 2359304 | tf_op jit(solution)/shard_map/ppermute | solution.py:373
  73.4 64.2 %copy-start.51 = (f32[768]{0:T(1024)}, f32[768]{0:T(1024)S(1)}, u32[]{:S(2)}) copy-start(f32[768]{0:T(1024)S(1)} %reshape.529) | copy-start | bytes 9220
  117.2 11.8 %copy-start.28 = (bf16[16,24,768]{2,1,0:T(8,128)(2,1)}, bf16[16,24,768]{2,1,0:T(8,128)(2,1)S(1)}, u32[]{:S(2)}) copy-start(bf16[16,24,768]{2,1,0:T(8,128)(2,1)S(1)} %slice.191) | copy-start | bytes 1769476
  117.3 14.8 %collective-permute-start.11 = (bf16[8,24,768]{2,1,0:T(8,128)(2,1)S(1)}, bf16[8,24,768]{2,1,0:T(8,128)(2,1)}, u32[]{:S(2)}, u32[]{:S(2)}) collective-permute-start(bf16[8,24,768]{2,1,0:T(8,128)(2,1)S(1)} %dynamic-slice_bitcast_fusion.3), channel_id=1, source_target_pairs={{0,1},{1,0},{2,3},{3,2},{4,5},{5,4},{6,7},{7,6},{8,9},{9,8},{10,11... | collective-permute-start | bytes 884744 | tf_op jit(solution)/shard_map/ppermute | solution.py:373
  134.5 5.0 %collective-permute-start.12 = (bf16[2,256,768]{2,1,0:T(8,128)(2,1)S(1)}, bf16[2,256,768]{2,1,0:T(8,128)(2,1)}, u32[]{:S(2)}, u32[]{:S(2)}) collective-permute-start(bf16[2,256,768]{2,1,0:T(8,128)(2,1)S(1)} %fusion.69), channel_id=1, source_target_pairs={{0,1},{1,0},{2,3},{3,2},{4,5},{5,4},{6,7},{7,6},{8,9},{9,8},{10,11... | collective-permute-start | bytes 2359304 | tf_op jit(solution)/shard_map/ppermute | solution.py:373
  143.7 20.7 %collective-permute-start.13 = (bf16[2,256,768]{2,1,0:T(8,128)(2,1)}, bf16[2,256,768]{2,1,0:T(8,128)(2,1)}, u32[]{:S(2)}, u32[]{:S(2)}) collective-permute-start(bf16[2,256,768]{2,1,0:T(8,128)(2,1)} %add_convert_fusion.1), channel_id=1, source_target_pairs={{0,1},{1,0},{2,3},{3,2},{4,5},{5,4},{6,7},{7,6},{8,9},{9,8},{10,11... | collective-permute-start | bytes 2359304 | tf_op jit(solution)/shard_map/ppermute | solution.py:373
  204.5 11.0 %collective-permute-start.14 = (bf16[2,256,768]{2,1,0:T(8,128)(2,1)S(1)}, bf16[2,256,768]{2,1,0:T(8,128)(2,1)S(1)}, u32[]{:S(2)}, u32[]{:S(2)}) collective-permute-start(bf16[2,256,768]{2,1,0:T(8,128)(2,1)S(1)} %fusion.72), channel_id=1, source_target_pairs={{0,1},{1,0},{2,3},{3,2},{4,5},{5,4},{6,7},{7,6},{8,9},{9,8},{10,11... | collective-permute-start | bytes 2359304 | tf_op jit(solution)/shard_map/ppermute | solution.py:373
  204.6 10.0 %collective-permute-start.18 = (bf16[2,256,768]{2,1,0:T(8,128)(2,1)S(1)}, bf16[2,256,768]{2,1,0:T(8,128)(2,1)S(1)}, u32[]{:S(2)}, u32[]{:S(2)}) collective-permute-start(bf16[2,256,768]{2,1,0:T(8,128)(2,1)S(1)} %fusion.70), channel_id=1, source_target_pairs={{0,1},{1,0},{2,3},{3,2},{4,5},{5,4},{6,7},{7,6},{8,9},{9,8},{10,11... | collective-permute-start | bytes 2359304 | tf_op jit(solution)/shard_map/ppermute | solution.py:373
  208.8 29.1 %collective-permute-start.32 = (bf16[4,2,48,1536]{3,2,1,0:T(8,128)(2,1)}, bf16[4,2,48,1536]{3,2,1,0:T(8,128)(2,1)}, u32[]{:S(2)}, u32[]{:S(2)}) collective-permute-start(bf16[4,2,48,1536]{3,2,1,0:T(8,128)(2,1)} %fusion.66), channel_id=1, source_target_pairs={{0,2},{2,0},{1,3},{3,1},{4,6},{6,4},{5,7},{7,5},{8,10},{10,8},{9,1... | collective-permute-start | bytes 3538952 | tf_op jit(solution)/shard_map/ppermute | solution.py:381
  218.0 27.4 %collective-permute-start.15 = (bf16[256,768]{1,0:T(8,128)(2,1)S(1)}, bf16[256,768]{1,0:T(8,128)(2,1)S(1)}, u32[]{:S(2)}, u32[]{:S(2)}) collective-permute-start(bf16[256,768]{1,0:T(8,128)(2,1)S(1)} %dynamic-slice_bitcast_fusion.1), channel_id=1, source_target_pairs={{0,2},{2,0},{1,3},{3,1},{4,6},{6,4},{5,7},{7,5},{8,10},{10,8},{9,1... | collective-permute-start | bytes 1179656 | tf_op jit(solution)/shard_map/ppermute | solution.py:381
  219.4 27.1 %collective-permute-start.19 = (bf16[2,256,768]{2,1,0:T(8,128)(2,1)}, bf16[2,256,768]{2,1,0:T(8,128)(2,1)S(1)}, u32[]{:S(2)}, u32[]{:S(2)}) collective-permute-start(bf16[2,256,768]{2,1,0:T(8,128)(2,1)} %get-tuple-element.44), channel_id=1, source_target_pairs={{0,1},{1,0},{2,3},{3,2},{4,5},{5,4},{6,7},{7,6},{8,9},{9,8},{10,11... | collective-permute-start | bytes 2359304 | tf_op jit(solution)/shard_map/ppermute | solution.py:373
  241.3 90.2 %collective-permute-start.33 = (bf16[4,48,1536]{2,1,0:T(8,128)(2,1)}, bf16[4,48,1536]{2,1,0:T(8,128)(2,1)}, u32[]{:S(2)}, u32[]{:S(2)}) collective-permute-start(bf16[4,48,1536]{2,1,0:T(8,128)(2,1)} %fusion.78), channel_id=1, source_target_pairs={{0,4},{4,0},{1,5},{5,1},{2,6},{6,2},{3,7},{7,3},{8,12},{12,8},{9,1... | collective-permute-start | bytes 1769480 | tf_op jit(solution)/shard_map/ppermute | solution.py:377
  249.6 13.3 %copy-start.73 = (bf16[1024,384]{0,1:T(8,128)(2,1)S(1)}, bf16[1024,384]{0,1:T(8,128)(2,1)}, u32[]{:S(2)}) copy-start(bf16[1024,384]{0,1:T(8,128)(2,1)} %add_convert_fusion.2) | copy-start | bytes 2359300
  323.0 13.4 %collective-permute-start.38 = (bf16[8,24,768]{2,1,0:T(8,128)(2,1)S(1)}, bf16[8,24,768]{2,1,0:T(8,128)(2,1)S(1)}, u32[]{:S(2)}, u32[]{:S(2)}) collective-permute-start(bf16[8,24,768]{2,1,0:T(8,128)(2,1)S(1)} %fusion.90), channel_id=1, source_target_pairs={{0,1},{1,0},{2,3},{3,2},{4,5},{5,4},{6,7},{7,6},{8,9},{9,8},{10,11... | collective-permute-start | bytes 884744 | tf_op jit(solution)/shard_map/ppermute | solution.py:373
  324.8 26.0 %collective-permute-start.20 = (bf16[2,256,768]{2,1,0:T(8,128)(2,1)S(1)}, bf16[2,256,768]{2,1,0:T(8,128)(2,1)S(1)}, u32[]{:S(2)}, u32[]{:S(2)}) collective-permute-start(bf16[2,256,768]{2,1,0:T(8,128)(2,1)S(1)} %fusion.71), channel_id=1, source_target_pairs={{0,1},{1,0},{2,3},{3,2},{4,5},{5,4},{6,7},{7,6},{8,9},{9,8},{10,11... | collective-permute-start | bytes 2359304 | tf_op jit(solution)/shard_map/ppermute | solution.py:373
  325.4 11.1 %slice-start = ((s8[4718592]{0:T(1024)(128)(4,1)}), s8[4194304]{0:T(1024)(128)(4,1)S(1)}, s32[]{:S(2)}) async-start(s8[4718592]{0:T(1024)(128)(4,1)} %bitcast.428), calls=%async_computation.1 | async-start | bytes 8388608
  325.5 11.1 %slice-start.1 = ((s8[4718592]{0:T(1024)(128)(4,1)}), s8[524288]{0:T(1024)(128)(4,1)S(1)}, s32[]{:S(2)}) async-start(s8[4718592]{0:T(1024)(128)(4,1)} %bitcast.428), calls=%async_computation.2 | async-start | bytes 1048576
  332.8 6.8 %collective-permute-start.34 = (bf16[48,1536]{1,0:T(8,128)(2,1)S(1)}, bf16[48,1536]{1,0:T(8,128)(2,1)S(1)}, u32[]{:S(2)}, u32[]{:S(2)}) collective-permute-start(bf16[48,1536]{1,0:T(8,128)(2,1)S(1)} %get-tuple-element.73), channel_id=1, source_target_pairs={{0,8},{8,0},{16,24},{24,16},{1,9},{9,1},{17,25},{25,17},{2,10},{10... | collective-permute-start | bytes 442376 | tf_op jit(solution)/shard_map/ppermute | solution.py:385
  334.2 10.0 %collective-permute-start.36 = (bf16[48,1536]{1,0:T(8,128)(2,1)S(1)}, bf16[48,1536]{1,0:T(8,128)(2,1)S(1)}, u32[]{:S(2)}, u32[]{:S(2)}) collective-permute-start(bf16[48,1536]{1,0:T(8,128)(2,1)S(1)} %get-tuple-element.74), channel_id=1, source_target_pairs={{0,24},{8,16},{16,8},{24,0},{1,25},{9,17},{17,9},{25,1},{2,26},{10... | collective-permute-start | bytes 442376 | tf_op jit(solution)/shard_map/ppermute | solution.py:385
  336.2 13.1 %collective-permute-start.35 = (bf16[48,1536]{1,0:T(8,128)(2,1)S(1)}, bf16[48,1536]{1,0:T(8,128)(2,1)S(1)}, u32[]{:S(2)}, u32[]{:S(2)}) collective-permute-start(bf16[48,1536]{1,0:T(8,128)(2,1)S(1)} %get-tuple-element.75), channel_id=1, source_target_pairs={{0,16},{8,24},{16,0},{24,8},{1,17},{9,25},{17,1},{25,9},{2,18},{10... | collective-permute-start | bytes 442376 | tf_op jit(solution)/shard_map/ppermute | solution.py:385
  336.6 14.2 %copy-start.1 = (bf16[1,256,768]{2,1,0:T(8,128)(2,1)S(1)}, bf16[1,256,768]{2,1,0:T(8,128)(2,1)}, u32[]{:S(2)}) copy-start(bf16[1,256,768]{2,1,0:T(8,128)(2,1)} %copy-done) | copy-start | bytes 1179652
  336.6 14.2 %copy-start.4 = (bf16[1,256,768]{2,1,0:T(8,128)(2,1)S(1)}, bf16[1,256,768]{2,1,0:T(8,128)(2,1)}, u32[]{:S(2)}) copy-start(bf16[1,256,768]{2,1,0:T(8,128)(2,1)} %copy-done.2) | copy-start | bytes 1179652
  336.6 14.2 %copy-start.30 = (f32[1024,768]{1,0:T(8,128)S(1)}, f32[1024,768]{1,0:T(8,128)}, u32[]{:S(2)}) copy-start(f32[1024,768]{1,0:T(8,128)} %fusion.42) | copy-start | bytes 9437188
  336.6 14.2 %copy-start.52 = (f32[768]{0:T(1024)S(1)}, f32[768]{0:T(1024)}, u32[]{:S(2)}) copy-start(f32[768]{0:T(1024)} %copy-done.51) | copy-start | bytes 9220
  336.7 14.2 %copy-start.58 = (f32[2,256]{1,0:T(2,128)S(1)}, f32[2,256]{1,0:T(2,128)}, u32[]{:S(2)}) copy-start(f32[2,256]{1,0:T(2,128)} %copy-done.57) | copy-start | bytes 6148
  336.7 14.2 %copy-start.59 = (f32[2,256]{1,0:T(2,128)S(1)}, f32[2,256]{1,0:T(2,128)}, u32[]{:S(2)}) copy-start(f32[2,256]{1,0:T(2,128)} %add_rsqrt_fusion.1) | copy-start | bytes 6148
  338.1 69.8 %collective-permute-start.39 = (bf16[4,2,120,768]{3,2,1,0:T(8,128)(2,1)}, bf16[4,2,120,768]{3,2,1,0:T(8,128)(2,1)}, u32[]{:S(2)}, u32[]{:S(2)}) collective-permute-start(bf16[4,2,120,768]{3,2,1,0:T(8,128)(2,1)} %fusion.58), channel_id=1, source_target_pairs={{0,4},{4,0},{1,5},{5,1},{2,6},{6,2},{3,7},{7,3},{8,12},{12,8},{9,1... | collective-permute-start | bytes 4423688 | tf_op jit(solution)/shard_map/ppermute | solution.py:377
  356.3 12.1 %collective-permute-start.21 = (bf16[256,768]{1,0:T(8,128)(2,1)S(1)}, bf16[256,768]{1,0:T(8,128)(2,1)S(1)}, u32[]{:S(2)}, u32[]{:S(2)}) collective-permute-start(bf16[256,768]{1,0:T(8,128)(2,1)S(1)} %fusion.81), channel_id=1, source_target_pairs={{0,2},{2,0},{1,3},{3,1},{4,6},{6,4},{5,7},{7,5},{8,10},{10,8},{9,1... | collective-permute-start | bytes 1179656 | tf_op jit(solution)/shard_map/ppermute | solution.py:381
  359.0 20.1 %collective-permute-start.22 = (bf16[4,2,56,576]{3,2,0,1:T(8,128)(2,1)S(1)}, bf16[4,2,56,576]{3,2,0,1:T(8,128)(2,1)S(1)}, u32[]{:S(2)}, u32[]{:S(2)}) collective-permute-start(bf16[4,2,56,576]{3,2,0,1:T(8,128)(2,1)S(1)} %fusion.80), channel_id=1, source_target_pairs={{0,2},{2,0},{1,3},{3,1},{4,6},{6,4},{5,7},{7,5},{8,10},{10,8},{9,1... | collective-permute-start | bytes 1548296 | tf_op jit(solution)/shard_map/ppermute | solution.py:381
  359.6 26.2 %collective-permute-start.27 = (bf16[4,2,56,576]{3,2,1,0:T(8,128)(2,1)S(1)}, bf16[4,2,56,576]{3,2,1,0:T(8,128)(2,1)S(1)}, u32[]{:S(2)}, u32[]{:S(2)}) collective-permute-start(bf16[4,2,56,576]{3,2,1,0:T(8,128)(2,1)S(1)} %fusion.79), channel_id=1, source_target_pairs={{0,4},{4,0},{1,5},{5,1},{2,6},{6,2},{3,7},{7,3},{8,12},{12,8},{9,1... | collective-permute-start | bytes 1548296 | tf_op jit(solution)/shard_map/ppermute | solution.py:377
  379.2 11.1 %collective-permute-start.23 = (bf16[4,56,576]{2,1,0:T(8,128)(2,1)S(1)}, bf16[4,56,576]{2,1,0:T(8,128)(2,1)S(1)}, u32[]{:S(2)}, u32[]{:S(2)}) collective-permute-start(bf16[4,56,576]{2,1,0:T(8,128)(2,1)S(1)} %fusion.95), channel_id=1, source_target_pairs={{0,4},{4,0},{1,5},{5,1},{2,6},{6,2},{3,7},{7,3},{8,12},{12,8},{9,1... | collective-permute-start | bytes 774152 | tf_op jit(solution)/shard_map/ppermute | solution.py:377
  386.0 8.5 %collective-permute-start.28 = (bf16[4,56,576]{2,1,0:T(8,128)(2,1)S(1)}, bf16[4,56,576]{2,1,0:T(8,128)(2,1)S(1)}, u32[]{:S(2)}, u32[]{:S(2)}) collective-permute-start(bf16[4,56,576]{2,1,0:T(8,128)(2,1)S(1)} %fusion.96), channel_id=1, source_target_pairs={{0,2},{2,0},{1,3},{3,1},{4,6},{6,4},{5,7},{7,5},{8,10},{10,8},{9,1... | collective-permute-start | bytes 774152 | tf_op jit(solution)/shard_map/ppermute | solution.py:381
  390.3 16.3 %copy-start.49 = (f32[24,1536]{1,0:T(8,128)S(1)}, f32[24,1536]{1,0:T(8,128)}, u32[]{:S(2)}) copy-start(f32[24,1536]{1,0:T(8,128)} %dynamic-slice_bitcast_fusion.4) | copy-start | bytes 442372
  390.3 17.6 %copy-start.7 = (f32[2,8,24,768]{3,2,1,0:T(8,128)S(1)}, f32[2,8,24,768]{3,2,1,0:T(8,128)}, u32[]{:S(2)}) copy-start(f32[2,8,24,768]{3,2,1,0:T(8,128)} %copy-done.6) | copy-start | bytes 3538948
  390.4 6.7 %collective-permute-start.24 = (bf16[56,576]{1,0:T(8,128)(2,1)S(1)}, bf16[56,576]{1,0:T(8,128)(2,1)S(1)}, u32[]{:S(2)}, u32[]{:S(2)}) collective-permute-start(bf16[56,576]{1,0:T(8,128)(2,1)S(1)} %get-tuple-element.90), channel_id=1, source_target_pairs={{0,8},{8,0},{16,24},{24,16},{1,9},{9,1},{17,25},{25,17},{2,10},{10... | collective-permute-start | bytes 193544 | tf_op jit(solution)/shard_map/ppermute | solution.py:385
  392.5 6.6 %collective-permute-start.26 = (bf16[56,576]{1,0:T(8,128)(2,1)S(1)}, bf16[56,576]{1,0:T(8,128)(2,1)S(1)}, u32[]{:S(2)}, u32[]{:S(2)}) collective-permute-start(bf16[56,576]{1,0:T(8,128)(2,1)S(1)} %get-tuple-element.91), channel_id=1, source_target_pairs={{0,24},{8,16},{16,8},{24,0},{1,25},{9,17},{17,9},{25,1},{2,26},{10... | collective-permute-start | bytes 193544 | tf_op jit(solution)/shard_map/ppermute | solution.py:385
  394.6 9.7 %collective-permute-start.25 = (bf16[56,576]{1,0:T(8,128)(2,1)S(1)}, bf16[56,576]{1,0:T(8,128)(2,1)S(1)}, u32[]{:S(2)}, u32[]{:S(2)}) collective-permute-start(bf16[56,576]{1,0:T(8,128)(2,1)S(1)} %get-tuple-element.92), channel_id=1, source_target_pairs={{0,16},{8,24},{16,0},{24,8},{1,17},{9,25},{17,1},{25,9},{2,18},{10... | collective-permute-start | bytes 193544 | tf_op jit(solution)/shard_map/ppermute | solution.py:385
  394.7 9.8 %collective-permute-start.29 = (bf16[56,576]{1,0:T(8,128)(2,1)S(1)}, bf16[56,576]{1,0:T(8,128)(2,1)S(1)}, u32[]{:S(2)}, u32[]{:S(2)}) collective-permute-start(bf16[56,576]{1,0:T(8,128)(2,1)S(1)} %get-tuple-element.93), channel_id=1, source_target_pairs={{0,8},{8,0},{16,24},{24,16},{1,9},{9,1},{17,25},{25,17},{2,10},{10... | collective-permute-start | bytes 193544 | tf_op jit(solution)/shard_map/ppermute | solution.py:385
  397.1 7.4 %collective-permute-start.31 = (bf16[56,576]{1,0:T(8,128)(2,1)S(1)}, bf16[56,576]{1,0:T(8,128)(2,1)S(1)}, u32[]{:S(2)}, u32[]{:S(2)}) collective-permute-start(bf16[56,576]{1,0:T(8,128)(2,1)S(1)} %get-tuple-element.94), channel_id=1, source_target_pairs={{0,24},{8,16},{16,8},{24,0},{1,25},{9,17},{17,9},{25,1},{2,26},{10... | collective-permute-start | bytes 193544 | tf_op jit(solution)/shard_map/ppermute | solution.py:385
  399.1 7.3 %collective-permute-start.30 = (bf16[56,576]{1,0:T(8,128)(2,1)S(1)}, bf16[56,576]{1,0:T(8,128)(2,1)S(1)}, u32[]{:S(2)}, u32[]{:S(2)}) collective-permute-start(bf16[56,576]{1,0:T(8,128)(2,1)S(1)} %get-tuple-element.95), channel_id=1, source_target_pairs={{0,16},{8,24},{16,0},{24,8},{1,17},{9,25},{17,1},{25,9},{2,18},{10... | collective-permute-start | bytes 193544 | tf_op jit(solution)/shard_map/ppermute | solution.py:385
  404.4 2.3 collective-permute-start.44
  406.6 6.9 %collective-permute-start.37 = (f32[24,2688]{1,0:T(8,128)S(1)}, f32[24,2688]{1,0:T(8,128)S(1)}, u32[]{:S(2)}, u32[]{:S(2)}) collective-permute-start(f32[24,2688]{1,0:T(8,128)S(1)} %pad_maximum_fusion.11), channel_id=1, source_target_pairs={{0,1},{1,0},{2,3},{3,2},{4,5},{5,4},{6,7},{7,6},{8,9},{9,8},{10,11... | collective-permute-start | bytes 774152 | tf_op jit(solution)/shard_map/ppermute | solution.py:373
  412.0 18.9 %collective-permute-start.40 = (bf16[4,120,768]{2,1,0:T(8,128)(2,1)S(1)}, bf16[4,120,768]{2,1,0:T(8,128)(2,1)S(1)}, u32[]{:S(2)}, u32[]{:S(2)}) collective-permute-start(bf16[4,120,768]{2,1,0:T(8,128)(2,1)S(1)} %fusion.75), channel_id=1, source_target_pairs={{0,2},{2,0},{1,3},{3,1},{4,6},{6,4},{5,7},{7,5},{8,10},{10,8},{9,1... | collective-permute-start | bytes 2211848 | tf_op jit(solution)/shard_map/ppermute | solution.py:381
  432.5 7.8 %collective-permute-start.41 = (bf16[120,768]{1,0:T(8,128)(2,1)S(1)}, bf16[120,768]{1,0:T(8,128)(2,1)S(1)}, u32[]{:S(2)}, u32[]{:S(2)}) collective-permute-start(bf16[120,768]{1,0:T(8,128)(2,1)S(1)} %get-tuple-element.68), channel_id=1, source_target_pairs={{0,8},{8,0},{16,24},{24,16},{1,9},{9,1},{17,25},{25,17},{2,10},{10... | collective-permute-start | bytes 552968 | tf_op jit(solution)/shard_map/ppermute | solution.py:385
  432.6 11.6 %collective-permute-start.43 = (bf16[120,768]{1,0:T(8,128)(2,1)S(1)}, bf16[120,768]{1,0:T(8,128)(2,1)S(1)}, u32[]{:S(2)}, u32[]{:S(2)}) collective-permute-start(bf16[120,768]{1,0:T(8,128)(2,1)S(1)} %get-tuple-element.69), channel_id=1, source_target_pairs={{0,24},{8,16},{16,8},{24,0},{1,25},{9,17},{17,9},{25,1},{2,26},{10... | collective-permute-start | bytes 552968 | tf_op jit(solution)/shard_map/ppermute | solution.py:385
  434.7 17.2 %collective-permute-start.42 = (bf16[120,768]{1,0:T(8,128)(2,1)S(1)}, bf16[120,768]{1,0:T(8,128)(2,1)S(1)}, u32[]{:S(2)}, u32[]{:S(2)}) collective-permute-start(bf16[120,768]{1,0:T(8,128)(2,1)S(1)} %get-tuple-element.70), channel_id=1, source_target_pairs={{0,16},{8,24},{16,0},{24,8},{1,17},{9,25},{17,1},{25,9},{2,18},{10... | collective-permute-start | bytes 552968 | tf_op jit(solution)/shard_map/ppermute | solution.py:385
  (58 other events, 228.9 us)
Sparse Core Ops, SparseCore 0:
  13.4 102.7 all-gather.2
